TPU v7x, 32 devices: a whole 2x2x4 slice. The times are simulated.
32 devices in a mesh: dp: 8 (over z, core), mp: 4 (over y, x).
Axes of the slice: x: 2, y: 2, z: 4, core: 2. Of those that a mesh axis runs over, the one named last changes fastest.
Arguments:
- inputs: bfloat16 [1024, 6144], P('dp', 'mp'), may hold values from -6 to 6
- up_weight: bfloat16 [4, 3, 24, 128, 128], P('mp'), may hold values from -0.3125 to 0.3125
- up_pick: int32 [4, 3, 24], P('mp'), may hold values from 0 to 11
- down_weight: bfloat16 [4, 3, 12, 2, 128, 128], P('mp'), may hold values from -0.21875 to 0.21875
- down_pick: int32 [4, 3, 12, 2], P('mp'), may hold values from 0 to 23
- cotangent: bfloat16 [1024, 6144], P('dp', 'mp'), may hold values from -6 to 6
Outputs:
- output: bfloat16 [1024, 6144], P('dp', 'mp')
- input_grad: bfloat16 [1024, 6144], P('dp', 'mp')
- up_grad: bfloat16 [4, 3, 24, 128, 128], P('mp')
- down_grad: bfloat16 [4, 3, 12, 2, 128, 128], P('mp')
All inputs are finite; a program needn't handle non-finite values.
Results may differ from a plain program's by a relative error of at most 0.005.
Values may be sent and summed in bfloat16 or wider, within the bound.
A program may use at most 64 MiB of HBM per device.

v0:
```python
import math

import jax
import jax.numpy as jnp
from jax import lax
from jax.sharding import PartitionSpec as P


def from_partner(block, axis, bit):
    count = lax.axis_size(axis)
    route = []
    for low in range(count):
        high = low | 1 << bit
        if high != low and high < count:
            route += [(low, high), (high, low)]
    return lax.ppermute(block, axis, route)


def select_blocks(source, chosen_ids, block_count):
    row_count = source.shape[0]
    blocks = source.reshape(row_count, block_count, -1)
    return jnp.take(blocks, chosen_ids, axis=1)


def place_blocks(partial_terms, chosen_ids, block_count):
    onehot = (chosen_ids[:, None] == jnp.arange(block_count, dtype=jnp.int32)[None, :]).astype(
        jnp.float32
    )
    return jnp.einsum("tmb,mn->tnb", partial_terms, onehot, precision=lax.Precision.HIGHEST)


def gelu_tanh(values_in):
    return jax.nn.gelu(values_in, approximate=True)


def local(inputs, up_weight, up_pick, down_weight, down_pick, cotangent):
    bit_count = lax.axis_size("mp").bit_length() - 1
    levels = bit_count + 1
    tokens, feature_width = inputs.shape
    in_blocks = down_weight.shape[2]
    hid_blocks = up_weight.shape[2]
    per_slot = down_weight.shape[3]
    block_size = up_weight.shape[3]
    grad_scale = 1.0 / math.sqrt(tokens * lax.axis_size("dp"))
    up_local = up_weight[0]
    up_ids = up_pick[0]
    down_local = down_weight[0]
    flat_ids = down_pick[0].reshape(levels, in_blocks * per_slot)
    sources = [inputs] + [from_partner(inputs, "mp", bit_num) for bit_num in range(bit_count)]
    picked_in = jnp.stack(
        [
            select_blocks(sources[level_num], up_ids[level_num], in_blocks)
            for level_num in range(levels)
        ],
        axis=1,
    )
    hidden = jnp.einsum("tlob,lobc->toc", picked_in, up_local, preferred_element_type=jnp.float32)
    activation = gelu_tanh(hidden).astype(jnp.bfloat16)
    act_flat = activation.reshape(tokens, hid_blocks * block_size)
    dy_blocks = cotangent.reshape(tokens, in_blocks, block_size)
    hidden_all = [act_flat] + [
        from_partner(act_flat, "mp", bit_num) for bit_num in range(bit_count)
    ]
    picked_hid = jnp.stack(
        [
            select_blocks(hidden_all[level_num], flat_ids[level_num], hid_blocks).reshape(
                tokens, in_blocks, per_slot, block_size
            )
            for level_num in range(levels)
        ],
        axis=1,
    )
    result = jnp.einsum(
        "tlokb,lokbc->toc", picked_hid, down_local, preferred_element_type=jnp.float32
    )
    down_part = jnp.einsum(
        "tlokb,toc->lokbc", picked_hid, dy_blocks, preferred_element_type=jnp.float32
    )
    back_terms = jnp.einsum(
        "toc,lokbc->tlokb", dy_blocks, down_local, preferred_element_type=jnp.float32
    )
    back_terms = back_terms.reshape(tokens, levels, in_blocks * per_slot, block_size)
    act_grad = place_blocks(back_terms[:, 0], flat_ids[0], hid_blocks)
    for bit_num in range(bit_count):
        placed = place_blocks(back_terms[:, bit_num + 1], flat_ids[bit_num + 1], hid_blocks)
        act_grad = act_grad + from_partner(placed, "mp", bit_num)
    _, gelu_back = jax.vjp(gelu_tanh, hidden)
    hidden_grad = gelu_back(act_grad)[0].astype(jnp.bfloat16)
    up_part = jnp.einsum(
        "tlob,toc->lobc", picked_in, hidden_grad, preferred_element_type=jnp.float32
    )
    in_terms = jnp.einsum(
        "toc,lobc->tlob", hidden_grad, up_local, preferred_element_type=jnp.float32
    )
    grad_inputs = place_blocks(in_terms[:, 0], up_ids[0], in_blocks)
    for bit_num in range(bit_count):
        placed = place_blocks(in_terms[:, bit_num + 1], up_ids[bit_num + 1], in_blocks)
        grad_inputs = grad_inputs + from_partner(placed, "mp", bit_num)
    up_sum, down_sum = lax.psum((up_part, down_part), "dp")
    up_out = (up_sum * grad_scale).astype(jnp.bfloat16)
    down_out = (down_sum * grad_scale).astype(jnp.bfloat16)
    return (
        result.reshape(tokens, feature_width).astype(jnp.bfloat16),
        grad_inputs.reshape(tokens, feature_width).astype(jnp.bfloat16),
        up_out[None],
        down_out[None],
    )


def solution(mesh):
    placed = (
        P("dp", "mp"),
        P("mp", None, None, None, None),
        P("mp", None, None),
        P("mp", None, None, None, None, None),
        P("mp", None, None, None),
        P("dp", "mp"),
    )
    return jax.shard_map(
        local,
        mesh=mesh,
        in_specs=placed,
        out_specs=(
            P("dp", "mp"),
            P("dp", "mp"),
            P("mp", None, None, None, None),
            P("mp", None, None, None, None, None),
        ),
        check_vma=False,
    )
```

profile of v0, /device:TPU:0, one launch (start us, length us, event | category | flops | bytes accessed | tf_op | source)
XLA Modules:
  0.0 335.1 jit_solution(7290400181199123162)
XLA Ops:
  9.3 3.0 collective-permute-start.1
  15.0 4.7 %fusion.8 = f32[128,3,12,2,128]{0,4,3,1,2:T(8,128)} fusion(bf16[128,12,128,1,1]{0,2,4,3,1:T(8,128)(2,1)S(1)} %bitcast.170, bf16[1,3,12,2,128,128]{5,4,3,2,1,0:T(8,128)(2,1)} %param.13), kind=kOutput, calls=%fused_computation.18 | convolution fusion | flops 301989888 | bytes 7471104 | tf_op jit(solution)/shard_map/toc,lokbc->tlokb/dot_general | solution.py:79
  19.7 6.1 %copy.200 = f32[128,3,12,2,128]{4,0,3,2,1:T(8,128)} copy(f32[128,3,12,2,128]{0,4,3,1,2:T(8,128)} %fusion.8) | data formatting | bytes 9437184 | tf_op jit(solution)/shard_map/toc,lokbc->tlokb/transpose | solution.py:79
  25.8 4.8 %fusion.73 = (f32[128,1,24,128]{3,0,2,1:T(8,128)}, f32[128,1,24,128]{3,0,2,1:T(8,128)}, f32[128,1,24,128]{3,0,2,1:T(8,128)}) fusion(f32[128,3,24,128]{3,0,2,1:T(8,128)} %bitcast.168), kind=kLoop, calls=%fused_computation.112 | loop fusion | bytes 9437184 | tf_op jit(solution)/shard_map/slice | solution.py:83
  30.7 4.2 %fusion.24 = f32[24,128,128]{2,0,1:T(8,128)} fusion(f32[128,1,24,128]{3,0,2,1:T(8,128)} %get-tuple-element.43, s32[24]{0:T(128)S(1)} %squeeze.49), kind=kOutput, calls=%fused_computation.38 | convolution fusion | flops 113246784 | bytes 3145824 | tf_op jit(solution)/shard_map/tmb,mn->tnb/dot_general | solution.py:29
  35.0 3.1 copy.206
  38.7 4.2 %fusion.25 = f32[24,128,128]{2,0,1:T(8,128)} fusion(f32[128,1,24,128]{3,0,2,1:T(8,128)} %get-tuple-element.42, s32[24]{0:T(128)S(1)} %squeeze.48), kind=kOutput, calls=%fused_computation.40 | convolution fusion | flops 113246784 | bytes 3145824 | tf_op jit(solution)/shard_map/tmb,mn->tnb/dot_general | solution.py:29
  42.9 3.0 copy.204
  50.2 4.3 %fusion.26 = f32[24,128,128]{2,0,1:T(8,128)} fusion(f32[128,1,24,128]{3,0,2,1:T(8,128)} %get-tuple-element.41, s32[24]{0:T(128)S(1)} %squeeze.47), kind=kOutput, calls=%fused_computation.42 | convolution fusion | flops 113246784 | bytes 3145824 | tf_op jit(solution)/shard_map/tmb,mn->tnb/dot_general | solution.py:29
  54.5 3.0 copy.202
  69.1 4.8 %collective-permute-done.5 = f32[128,24,128]{0,2,1:T(8,128)} collective-permute-done((f32[128,24,128]{0,2,1:T(8,128)}, f32[128,24,128]{0,2,1:T(8,128)}, u32[]{:S(2)}, u32[]{:S(2)}) %collective-permute-start.5) | collective-permute-done | bytes 1572896 | tf_op jit(solution)/shard_map/ppermute | solution.py:16
  73.9 7.7 %collective-permute-done.4 = f32[128,24,128]{0,2,1:T(8,128)} collective-permute-done((f32[128,24,128]{0,2,1:T(8,128)}, f32[128,24,128]{0,2,1:T(8,128)}, u32[]{:S(2)}, u32[]{:S(2)}) %collective-permute-start.4) | collective-permute-done | bytes 1572896 | tf_op jit(solution)/shard_map/ppermute | solution.py:16
  81.6 4.4 %fusion.23 = (bf16[128,24,128]{0,2,1:T(8,128)(2,1)}, bf16[128,24,128]{0,2,1:T(8,128)(2,1)}) fusion(f32[128,24,128]{0,2,1:T(8,128)} %collective-permute-done.5, f32[128,24,128]{0,2,1:T(8,128)} %collective-permute-done.4, f32[24,128,128]{1,2,0:T(8,128)S(1)} %copy-done.8, bf16[128,1,24,128]{3,0,1,2:T(8,128)(2,1)S(1)} %get-tuple-element.56, ...), kind=kOutput, calls=%fused_computation.33 | convolution fusion | flops 313786368 | bytes 11010048 | tf_op jit(solution)/shard_map/tlob,lobc->toc/dot_general | solution.py:57
  93.4 4.8 %convolution_bitcast_fusion = f32[3,24,128,128]{2,3,0,1:T(8,128)} fusion(bf16[128,1,24,128]{3,0,1,2:T(8,128)(2,1)} %copy-done.2, bf16[128,1,24,128]{3,0,1,2:T(8,128)(2,1)} %copy-done.3, bf16[128,1,24,128]{3,0,1,2:T(8,128)(2,1)} %select_bitcast_fusion.2, bf16[128,24,128]{0,2,1:T(8,128)(2,1)} %get-tuple-element.44), kind=kOutput, calls=%fused_computation.20 | convolution fusion | flops 309067776 | bytes 7864320 | tf_op jit(solution)/shard_map/tlob,toc->lobc/dot_general | solution.py:89
  98.1 5.8 %collective-permute-done.3 = bf16[128,3072]{0,1:T(8,128)(2,1)} collective-permute-done((bf16[128,3072]{0,1:T(8,128)(2,1)}, bf16[128,3072]{0,1:T(8,128)(2,1)}, u32[]{:S(2)}, u32[]{:S(2)}) %collective-permute-start.3) | collective-permute-done | bytes 786464 | tf_op jit(solution)/shard_map/ppermute | solution.py:16
  105.4 2.3 copy.190
  114.4 4.4 %fusion.11 = f32[3,12,2,128,128]{4,3,2,0,1:T(8,128)} fusion(bf16[128,12,128,1,1]{0,2,4,3,1:T(8,128)(2,1)S(1)} %bitcast.171, bf16[128,1,12,2,128]{4,0,1,2,3:T(8,128)(2,1)} %copy.193, bf16[128,1,12,2,128]{4,0,3,2,1:T(8,128)(2,1)S(1)} %bitcast.177, bf16[128,1,12,2,128]{4,0,3,2,1:T(8,128)(2,1)} %bitcast.175), kind=kOutput, calls=%fused_computation.19 | convolution fusion | flops 309067776 | bytes 7471104 | tf_op jit(solution)/shard_map/tlokb,toc->lokbc/dot_general | solution.py:76
  134.3 6.9 %collective-permute-done.7 = f32[128,12,128]{2,0,1:T(8,128)} collective-permute-done((f32[128,12,128]{2,0,1:T(8,128)}, f32[128,12,128]{2,0,1:T(8,128)}, u32[]{:S(2)}, u32[]{:S(2)}) %collective-permute-start.7) | collective-permute-done | bytes 786464 | tf_op jit(solution)/shard_map/ppermute | solution.py:16
  141.2 4.0 %collective-permute-done.6 = f32[128,12,128]{2,0,1:T(8,128)} collective-permute-done((f32[128,12,128]{2,0,1:T(8,128)}, f32[128,12,128]{2,0,1:T(8,128)}, u32[]{:S(2)}, u32[]{:S(2)}) %collective-permute-start.6) | collective-permute-done | bytes 786464 | tf_op jit(solution)/shard_map/ppermute | solution.py:16
  145.3 2.4 fusion.52
  149.8 165.1 %all-reduce.3.cloned.1.call-done = (f32[3,24,128,128]{2,3,0,1:T(8,128)}, f32[3,12,2,128,128]{4,3,2,0,1:T(8,128)}) async-done(((f32[3,24,128,128]{2,3,0,1:T(8,128)}, f32[3,12,2,128,128]{4,3,2,0,1:T(8,128)}), (f32[3,24,128,128]{2,3,0,1:T(8,128)}, f32[3,12,2,128,128]{4,3,2,0,1:T(8,128)})) %all-reduce.3.cloned.1.call-update) | async-done | bytes 9437200 | tf_op jit(solution)/shard_map/psum | solution.py:99
  315.0 4.3 %fusion = bf16[1,3,24,128,128]{3,4,1,2,0:T(8,128)(2,1)} fusion(f32[3,24,128,128]{2,3,0,1:T(8,128)} %get-tuple-element.30), kind=kLoop, calls=%fused_computation.8 | loop fusion | flops 2359296 | bytes 7077888 | tf_op jit(solution)/shard_map/broadcast_in_dim | solution.py:105
  319.3 4.3 %copy.220 = bf16[1,3,24,128,128]{4,3,2,1,0:T(8,128)(2,1)} copy(bf16[1,3,24,128,128]{3,4,1,2,0:T(8,128)(2,1)} %fusion) | data formatting | bytes 4718592
  323.6 2.9 fusion.1
  (107 shorter events, 56.2 us)
Async XLA Ops:
  7.2 74.4 %copy-start = (bf16[1,3,24,128,128]{4,3,2,1,0:T(8,128)(2,1)S(1)}, bf16[1,3,24,128,128]{4,3,2,1,0:T(8,128)(2,1)}, u32[]{:S(2)}) copy-start(bf16[1,3,24,128,128]{4,3,2,1,0:T(8,128)(2,1)} %param.11) | copy-start | bytes 7077892
  7.2 307.8 %all-reduce.3.cloned.1.call-start = ((), (), s32[]{:S(2)}) async-start(), calls=%async_computation | async-start | bytes 18874368 | tf_op jit(solution)/shard_map/psum | solution.py:99
  9.3 52.5 %collective-permute-start.1 = (bf16[128,1536]{0,1:T(8,128)(2,1)}, bf16[128,1536]{0,1:T(8,128)(2,1)}, u32[]{:S(2)}, u32[]{:S(2)}) collective-permute-start(bf16[128,1536]{0,1:T(8,128)(2,1)} %copy.182), channel_id=1, source_target_pairs={{0,2},{2,0},{1,3},{3,1},{4,6},{6,4},{5,7},{7,5},{8,10},{10,8},{9,1... | collective-permute-start | bytes 1179656 | tf_op jit(solution)/shard_map/ppermute | solution.py:16
  12.3 50.8 %collective-permute-start = (bf16[128,1536]{0,1:T(8,128)(2,1)}, bf16[128,1536]{0,1:T(8,128)(2,1)}, u32[]{:S(2)}, u32[]{:S(2)}) collective-permute-start(bf16[128,1536]{0,1:T(8,128)(2,1)} %copy.182), channel_id=1, source_target_pairs={{0,1},{1,0},{2,3},{3,2},{4,5},{5,4},{6,7},{7,6},{8,9},{9,8},{10,11... | collective-permute-start | bytes 1179656 | tf_op jit(solution)/shard_map/ppermute | solution.py:16
  38.0 35.9 %collective-permute-start.5 = (f32[128,24,128]{0,2,1:T(8,128)}, f32[128,24,128]{0,2,1:T(8,128)}, u32[]{:S(2)}, u32[]{:S(2)}) collective-permute-start(f32[128,24,128]{0,2,1:T(8,128)} %bitcast.172), channel_id=1, source_target_pairs={{0,2},{2,0},{1,3},{3,1},{4,6},{6,4},{5,7},{7,5},{8,10},{10,8},{9,1... | collective-permute-start | bytes 4718600 | tf_op jit(solution)/shard_map/ppermute | solution.py:16
  42.9 5.5 %copy-start.13 = (s32[1,3,24]{2,0,1:T(1,128)S(1)}, s32[1,3,24]{2,0,1:T(1,128)}, u32[]{:S(2)}) copy-start(s32[1,3,24]{2,0,1:T(1,128)} %param.12) | copy-start | bytes 868
  46.0 35.6 %collective-permute-start.4 = (f32[128,24,128]{0,2,1:T(8,128)}, f32[128,24,128]{0,2,1:T(8,128)}, u32[]{:S(2)}, u32[]{:S(2)}) collective-permute-start(f32[128,24,128]{0,2,1:T(8,128)} %bitcast.173), channel_id=1, source_target_pairs={{0,1},{1,0},{2,3},{3,2},{4,5},{5,4},{6,7},{7,6},{8,9},{9,8},{10,11... | collective-permute-start | bytes 4718600 | tf_op jit(solution)/shard_map/ppermute | solution.py:16
  61.8 5.6 %copy-start.15 = (pred[24]{0:T(512)(128)(4,1)S(1)}, pred[24]{0:T(512)(128)(4,1)}, u32[]{:S(2)}) copy-start(pred[24]{0:T(512)(128)(4,1)} %get-tuple-element.52) | copy-start | bytes 76
  61.8 5.6 %copy-start.16 = (pred[24]{0:T(512)(128)(4,1)S(1)}, pred[24]{0:T(512)(128)(4,1)}, u32[]{:S(2)}) copy-start(pred[24]{0:T(512)(128)(4,1)} %get-tuple-element.54) | copy-start | bytes 76
  67.4 14.2 %copy-start.1 = (bf16[128,1,24,128]{3,0,1,2:T(8,128)(2,1)S(1)}, bf16[128,1,24,128]{3,0,1,2:T(8,128)(2,1)}, u32[]{:S(2)}) copy-start(bf16[128,1,24,128]{3,0,1,2:T(8,128)(2,1)} %select_bitcast_fusion.2) | copy-start | bytes 2359300
  67.4 14.2 %copy-start.8 = (f32[24,128,128]{1,2,0:T(8,128)S(1)}, f32[24,128,128]{1,2,0:T(8,128)}, u32[]{:S(2)}) copy-start(f32[24,128,128]{1,2,0:T(8,128)} %copy.202) | copy-start | bytes 4718596
  69.1 16.9 %copy-start.2 = (bf16[128,1,24,128]{3,0,1,2:T(8,128)(2,1)}, bf16[128,1,24,128]{3,0,1,2:T(8,128)(2,1)S(1)}, u32[]{:S(2)}) copy-start(bf16[128,1,24,128]{3,0,1,2:T(8,128)(2,1)S(1)} %get-tuple-element.56) | copy-start | bytes 2359300
  69.1 16.9 %copy-start.3 = (bf16[128,1,24,128]{3,0,1,2:T(8,128)(2,1)}, bf16[128,1,24,128]{3,0,1,2:T(8,128)(2,1)S(1)}, u32[]{:S(2)}) copy-start(bf16[128,1,24,128]{3,0,1,2:T(8,128)(2,1)S(1)} %get-tuple-element.57) | copy-start | bytes 2359300
  81.6 6.5 %copy-start.20 = (s32[24]{0:T(128)S(1)}, s32[24]{0:T(128)}, u32[]{:S(2)}) copy-start(s32[24]{0:T(128)} %compare_select_fusion) | copy-start | bytes 292
  81.6 6.5 %copy-start.21 = (s32[24]{0:T(128)S(1)}, s32[24]{0:T(128)}, u32[]{:S(2)}) copy-start(s32[24]{0:T(128)} %compare_select_fusion.1) | copy-start | bytes 292
  81.6 8.4 %copy-start.19 = (pred[24]{0:T(512)(128)(4,1)S(1)}, pred[24]{0:T(512)(128)(4,1)}, u32[]{:S(2)}) copy-start(pred[24]{0:T(512)(128)(4,1)} %compare_and_fusion.2) | copy-start | bytes 76
  86.0 17.9 %collective-permute-start.3 = (bf16[128,3072]{0,1:T(8,128)(2,1)}, bf16[128,3072]{0,1:T(8,128)(2,1)}, u32[]{:S(2)}, u32[]{:S(2)}) collective-permute-start(bf16[128,3072]{0,1:T(8,128)(2,1)} %bitcast.19), channel_id=1, source_target_pairs={{0,2},{2,0},{1,3},{3,1},{4,6},{6,4},{5,7},{7,5},{8,10},{10,8},{9,1... | collective-permute-start | bytes 2359304 | tf_op jit(solution)/shard_map/ppermute | solution.py:16
  87.6 17.8 %collective-permute-start.2 = (bf16[128,3072]{0,1:T(8,128)(2,1)}, bf16[128,3072]{0,1:T(8,128)(2,1)}, u32[]{:S(2)}, u32[]{:S(2)}) collective-permute-start(bf16[128,3072]{0,1:T(8,128)(2,1)} %bitcast.19), channel_id=1, source_target_pairs={{0,1},{1,0},{2,3},{3,2},{4,5},{5,4},{6,7},{7,6},{8,9},{9,8},{10,11... | collective-permute-start | bytes 2359304 | tf_op jit(solution)/shard_map/ppermute | solution.py:16
  103.9 5.4 %copy-start.17 = (pred[24]{0:T(512)(128)(4,1)S(1)}, pred[24]{0:T(512)(128)(4,1)}, u32[]{:S(2)}) copy-start(pred[24]{0:T(512)(128)(4,1)} %compare_and_fusion) | copy-start | bytes 76
  107.7 5.6 %copy-start.18 = (pred[24]{0:T(512)(128)(4,1)S(1)}, pred[24]{0:T(512)(128)(4,1)}, u32[]{:S(2)}) copy-start(pred[24]{0:T(512)(128)(4,1)} %compare_and_fusion.1) | copy-start | bytes 76
  109.3 5.1 %copy-start.7 = (bf16[128,1536]{0,1:T(8,128)(2,1)S(1)}, bf16[128,1536]{0,1:T(8,128)(2,1)}, u32[]{:S(2)}) copy-start(bf16[128,1536]{0,1:T(8,128)(2,1)} %copy-done.6) | copy-start | bytes 1179652
  124.3 16.9 %collective-permute-start.7 = (f32[128,12,128]{2,0,1:T(8,128)}, f32[128,12,128]{2,0,1:T(8,128)}, u32[]{:S(2)}, u32[]{:S(2)}) collective-permute-start(f32[128,12,128]{2,0,1:T(8,128)} %copy.214), channel_id=1, source_target_pairs={{0,2},{2,0},{1,3},{3,1},{4,6},{6,4},{5,7},{7,5},{8,10},{10,8},{9,1... | collective-permute-start | bytes 2359304 | tf_op jit(solution)/shard_map/ppermute | solution.py:16
  125.8 4.9 %copy-start.12 = (bf16[24,128,128]{2,1,0:T(8,128)(2,1)S(1)}, bf16[24,128,128]{2,1,0:T(8,128)(2,1)}, u32[]{:S(2)}) copy-start(bf16[24,128,128]{2,1,0:T(8,128)(2,1)} %copy-done.11) | copy-start | bytes 2359300
  128.6 16.6 %collective-permute-start.6 = (f32[128,12,128]{2,0,1:T(8,128)}, f32[128,12,128]{2,0,1:T(8,128)}, u32[]{:S(2)}, u32[]{:S(2)}) collective-permute-start(f32[128,12,128]{2,0,1:T(8,128)} %copy.212), channel_id=1, source_target_pairs={{0,1},{1,0},{2,3},{3,2},{4,5},{5,4},{6,7},{7,6},{8,9},{9,8},{10,11... | collective-permute-start | bytes 2359304 | tf_op jit(solution)/shard_map/ppermute | solution.py:16
  (7 other events, 21.5 us)
Sparse Core Ops, SparseCore 0:
  118.9 196.0 all-reduce.2
where the time goes:
time: 336 us; the launch traced here: 335 us
  waiting for transfers between devices  194 us (58%)
  local copies, waits for them, and re-layouts  57.5 us (17%)
  matrix products  38.5 us (11%)
  other arithmetic  21.2 us (6%)
  between operations  14.4 us (4%)
  starting transfers between devices  9.2 us (3%)
    psum x1, waiting for transfers between devices, local(): up_sum, down_sum = lax.psum((up_part, down_part), 'dp')  165 us
    ppermute x8, waiting for transfers between devices, from_partner(): return lax.ppermute(block, axis, route)  29.2 us
    dot_general x6, matrix products, place_blocks(): jnp.einsum('tmb,mn->tnb', partial_terms, onehot, precision=lax.Precision....  17.5 us
    unnamed x50, local copies, waits for them, and re-layouts  14.2 us
    ppermute x8, starting transfers between devices, from_partner(): return lax.ppermute(block, axis, route)  9.16 us
    dot_general x3, local copies, waits for them, and re-layouts, place_blocks(): jnp.einsum('tmb,mn->tnb', partial_terms, onehot, precision=lax.Precision....  9.13 us
    gather x6, local copies, waits for them, and re-layouts, select_blocks(): return jnp.take(blocks, chosen_ids, axis=1)  9.06 us
    reshape x5, local copies, waits for them, and re-layouts, select_blocks(): blocks = source.reshape(row_count, block_count, -1)  7.47 us
  transfers between devices with their start and end apart: 9, of which 6 were waited for; matrix products, arithmetic and copies ran while one was open for 25% of the time, Pallas kernels for 0%

commit v1 on v0

v1 whole, which is shorter than its diff:
```python
import functools
import math

import jax
import jax.numpy as jnp
from jax import lax
from jax.experimental import pallas as pl
from jax.experimental.pallas import tpu as pltpu
from jax.sharding import PartitionSpec as P

F32 = jnp.float32
BF16 = jnp.bfloat16
VM = pl.BlockSpec(memory_space=pltpu.VMEM)
SM = pl.BlockSpec(memory_space=pltpu.SMEM)


def dot(a, b, dims):
    return lax.dot_general(a, b, (dims, ((), ())), preferred_element_type=F32)


def call(body, outs, flops, moved, in_specs, scratch=()):
    return pl.pallas_call(
        body,
        out_shape=[jax.ShapeDtypeStruct(s, d) for s, d in outs],
        in_specs=in_specs,
        out_specs=[VM] * len(outs),
        scratch_shapes=list(scratch),
        compiler_params=pltpu.CompilerParams(vmem_limit_bytes=48 * 2**20),
        cost_estimate=pl.CostEstimate(flops=flops, bytes_accessed=moved, transcendentals=0),
    )


def columns(block, size):
    return pl.ds(pl.multiple_of(block * size, size), size)


def back_body(levels, pick, dy, weight, *rest):
    outs, total = rest[:levels], rest[levels]
    _, _, out_blocks, slots, size, _ = weight.shape
    total[...] = jnp.zeros_like(total)

    @pl.loop(0, out_blocks)
    def _(o):
        grad = dy[:, columns(o, size)]
        terms = [
            (l, k, dot(grad, weight[0, l, o, k], ((1,), (1,))))
            for l in range(levels)
            for k in range(slots)
        ]
        for l, k, term in terms:
            spot = pick[0, l, o, k]
            total[l, spot] += term

    for l in range(levels):
        outs[l][...] = total[l].astype(outs[l].dtype)


def gelu_parts(v):
    c = 0.7978845608028654
    t = jnp.tanh(c * (v + 0.044715 * (v * v * v)))
    return t, c


def up_body(levels, pick, *rest):
    sources, weight, hidden, act = rest[:levels], rest[levels], rest[levels + 1], rest[levels + 2]
    hid_blocks, size = weight.shape[2], weight.shape[3]

    def one(o):
        acc = None
        for l in range(levels):
            block = sources[l][:, columns(pick[0, l, o], size)]
            term = dot(block, weight[0, l, o], ((1,), (0,)))
            acc = term if acc is None else acc + term
        t, _ = gelu_parts(acc)
        hidden[o] = acc
        act[o] = (0.5 * acc * (1.0 + t)).astype(BF16)

    @pl.loop(0, hid_blocks // 3)
    def _(step):
        for i in range(3):
            one(step * 3 + i)


def mid_body(levels, pick, *rest):
    sources = rest[:levels]
    weight, hidden = rest[levels], rest[levels + 1]
    grads = rest[levels + 2 : 2 * levels + 2]
    up_part = rest[2 * levels + 2]
    outs = rest[2 * levels + 3 : 3 * levels + 3]
    total, flipped = rest[3 * levels + 3 :]
    hid_blocks, size = weight.shape[2], weight.shape[3]
    in_blocks = sources[0].shape[1] // size
    total[...] = jnp.zeros_like(total)

    @pl.loop(0, in_blocks)
    def _(b):
        for l in range(levels):
            flipped[l, b] = sources[l][:, columns(b, size)].T

    def one(o):
        v = hidden[o]
        grad = grads[0][o]
        for l in range(1, levels):
            grad = grad + grads[l][o].astype(F32)
        t, c = gelu_parts(v)
        slope = 0.5 * (1.0 + t) + 0.5 * v * (1.0 - t * t) * (c * (1.0 + 3 * 0.044715 * (v * v)))
        hg = (grad * slope).astype(BF16)
        terms = []
        for l in range(levels):
            up_part[l, o] = dot(flipped[l, pick[0, l, o]], hg, ((1,), (0,))).astype(BF16)
            terms.append(dot(hg, weight[0, l, o], ((1,), (1,))))
        return terms

    @pl.loop(0, hid_blocks // 2)
    def _(step):
        both = [one(step * 2 + i) for i in range(2)]
        for i in range(2):
            for l in range(levels):
                spot = pick[0, l, step * 2 + i]
                total[l, spot] += both[i][l]

    for l in range(levels):
        outs[l][...] = total[l].astype(outs[l].dtype)


def down_body(levels, pick, *rest):
    acts, weight, dy, result, down_part = rest[:levels], *rest[levels:]
    _, _, out_blocks, slots, size, _ = weight.shape

    @pl.loop(0, out_blocks)
    def _(o):
        grad = dy[:, columns(o, size)]
        acc = None
        for l in range(levels):
            for k in range(slots):
                act = acts[l][pick[0, l, o, k]]
                term = dot(act, weight[0, l, o, k], ((1,), (0,)))
                acc = term if acc is None else acc + term
                down_part[l, o, k] = dot(act, grad, ((0,), (0,))).astype(BF16)
        result[:, columns(o, size)] = acc.astype(BF16)


def sum_body(levels, *rest):
    terms, out = rest[:levels], rest[levels]
    blocks, _, size = terms[0].shape

    for b in range(blocks):
        acc = terms[0][b]
        for l in range(1, levels):
            acc = acc + terms[l][b].astype(F32)
        out[:, b * size : (b + 1) * size] = acc.astype(BF16)


def swap(block, axis, bit):
    count = lax.axis_size(axis)
    return lax.ppermute(block, axis, [(i, i ^ (1 << bit)) for i in range(count)])


def token_sum(part, scale):
    me = lax.axis_index("dp")
    bits = lax.axis_size("dp").bit_length() - 1
    value = part.reshape(-1, part.shape[-1])
    for bit in range(bits):
        mine = (me >> bit) & 1
        rows = value.shape[0] // 2
        sent = lax.dynamic_slice_in_dim(value, (1 - mine) * rows, rows).astype(BF16)
        kept = lax.dynamic_slice_in_dim(value, mine * rows, rows).astype(F32)
        value = kept + swap(sent, "dp", bit).astype(F32)
    value = (value * scale).astype(BF16)
    for bit in reversed(range(bits)):
        mine = (me >> bit) & 1
        other = swap(value, "dp", bit)
        first = jnp.where(mine == 0, value, other)
        last = jnp.where(mine == 0, other, value)
        value = jnp.concatenate([first, last], axis=0)
    return value.reshape((1,) + part.shape)


def local(inputs, up_weight, up_pick, down_weight, down_pick, cotangent):
    bit_count = lax.axis_size("mp").bit_length() - 1
    levels = bit_count + 1
    tokens, width = inputs.shape
    in_blocks, slots = down_weight.shape[2:4]
    hid_blocks, size = up_weight.shape[2:4]
    scale = 1.0 / math.sqrt(tokens * lax.axis_size("dp"))
    macs = 2 * levels * hid_blocks * tokens * size * size
    hid = (hid_blocks, tokens, size)
    feat = (in_blocks, tokens, size)

    sources = [inputs] + [swap(inputs, "mp", b) for b in range(bit_count)]
    placed = call(
        functools.partial(back_body, levels),
        [(hid, F32)] + [(hid, BF16)] * bit_count,
        macs, 8 * 2**20, [SM, VM, VM],
        [pltpu.VMEM((levels,) + hid, F32)],
    )(down_pick, cotangent, down_weight)
    grads = [placed[0]] + [swap(placed[b + 1], "mp", b) for b in range(bit_count)]
    hidden, act = call(
        functools.partial(up_body, levels),
        [(hid, F32), (hid, BF16)],
        macs, 8 * 2**20, [SM] + [VM] * (levels + 1),
    )(up_pick, *sources, up_weight)
    acts = [act] + [swap(act, "mp", b) for b in range(bit_count)]
    mid = call(
        functools.partial(mid_body, levels),
        [((levels, hid_blocks, size, size), BF16), (feat, F32)] + [(feat, BF16)] * bit_count,
        2 * macs, 16 * 2**20, [SM] + [VM] * (2 * levels + 2),
        [
            pltpu.VMEM((levels,) + feat, F32),
            pltpu.VMEM((levels, in_blocks, size, tokens), BF16),
        ],
    )(up_pick, *sources, up_weight, hidden, *grads)
    up_part, back = mid[0], mid[1:]
    result, down_part = call(
        functools.partial(down_body, levels),
        [((tokens, width), BF16), ((levels, in_blocks, slots, size, size), BF16)],
        2 * macs, 12 * 2**20, [SM] + [VM] * (levels + 2),
    )(down_pick, *acts, down_weight, cotangent)
    backs = [back[0]] + [swap(back[b + 1], "mp", b) for b in range(bit_count)]
    up_out = token_sum(up_part, scale)
    down_out = token_sum(down_part, scale)
    [grad_inputs] = call(
        functools.partial(sum_body, levels),
        [((tokens, width), BF16)], 2**20, 2 * 2**20, [VM] * levels,
    )(*backs)
    return result, grad_inputs, up_out, down_out


def solution(mesh):
    placed = (
        P("dp", "mp"),
        P("mp", None, None, None, None),
        P("mp", None, None),
        P("mp", None, None, None, None, None),
        P("mp", None, None, None),
        P("dp", "mp"),
    )
    return jax.shard_map(
        local,
        mesh=mesh,
        in_specs=placed,
        out_specs=(
            P("dp", "mp"),
            P("dp", "mp"),
            P("mp", None, None, None, None),
            P("mp", None, None, None, None, None),
        ),
        check_vma=False,
    )
```

time: 336 us -> 192 us (0.57)
  waiting for transfers between devices: 194 us -> 92.6 us
  local copies, waits for them, and re-layouts: 57.5 us -> 10.1 us
  matrix products: 38.5 us -> 0 us
  Pallas kernels: 0 us -> 26 us
  starting transfers between devices: 9.2 us -> 34 us
  between operations: 14.4 us -> 0.9 us
    psum x1 -> x0, waiting for transfers between devices: 165 us -> none  [local(): up_sum, down_sum = lax.psum((up_part, down_part), 'dp')]
    ppermute x8 -> x20, waiting for transfers between devices: 29.2 us -> 92.6 us  [swap(): return lax.ppermute(block, axis, [(i, i ^ 1 << bit) for i in range(count)])]
    dot_general x12 -> x0, matrix products: 38.5 us -> none  [the longest x6 17.5 us: place_blocks(): jnp.einsum('tmb,mn->tnb', partial_terms, onehot, precision=lax.Precision....]
    pallas_call x0 -> x5, Pallas kernels: none -> 26 us  [the longest x1 9.86 us: local(): call(functools.partial(mid_body, levels), [((levels, hid_blocks, size, si...]
    ppermute x8 -> x20, starting transfers between devices: 9.16 us -> 34 us  [swap(): return lax.ppermute(block, axis, [(i, i ^ 1 << bit) for i in range(count)])]
    concatenate x0 -> x6, other arithmetic: none -> 18.9 us  [token_sum(): value = jnp.concatenate([first, last], axis=0)]
    dot_general x3 -> x0, local copies, waits for them, and re-layouts: 9.13 us -> none  [place_blocks(): jnp.einsum('tmb,mn->tnb', partial_terms, onehot, precision=lax.Precision....]
    gather x6 -> x0, local copies, waits for them, and re-layouts: 9.06 us -> none  [select_blocks(): return jnp.take(blocks, chosen_ids, axis=1)]
  transfers between devices with their start and end apart: 9 -> 20, of which waited for: 6 -> 11; matrix products, arithmetic and copies ran while one was open for 25% -> 10% of each run, Pallas kernels for 0% -> 11%
where the time goes in v1:
time: 192 us; the launch traced here: 188 us
  waiting for transfers between devices  92.6 us (48%)
  starting transfers between devices  34 us (18%)
  Pallas kernels  26 us (14%)
  other arithmetic  24.5 us (13%)
  local copies, waits for them, and re-layouts  10.1 us (5%)
    ppermute x20, waiting for transfers between devices, swap(): return lax.ppermute(block, axis, [(i, i ^ 1 << bit) for i in range(count)])  92.6 us
    ppermute x20, starting transfers between devices, swap(): return lax.ppermute(block, axis, [(i, i ^ 1 << bit) for i in range(count)])  34 us
    concatenate x6, other arithmetic, token_sum(): value = jnp.concatenate([first, last], axis=0)  18.9 us
    pallas_call x1, Pallas kernels, local(): call(functools.partial(mid_body, levels), [((levels, hid_blocks, size, si...  9.86 us
    unnamed x34, local copies, waits for them, and re-layouts  6.14 us
    pallas_call x1, Pallas kernels, local(): call(functools.partial(down_body, levels), [((tokens, width), BF16), ((le...  6.03 us
    pallas_call x1, Pallas kernels, local(): call(functools.partial(back_body, levels), [(hid, F32)] + [(hid, BF16)] *...  5.66 us
  transfers between devices with their start and end apart: 20, of which 11 were waited for; matrix products, arithmetic and copies ran while one was open for 10% of the time, Pallas kernels for 11%

profile of v1, /device:TPU:0, one launch (start us, length us, event | category | flops | bytes accessed | tf_op | source)
XLA Modules:
  0.0 188.0 jit_solution(216482755768639034)
XLA Ops:
  1.4 1.7 copy-done.1
  4.1 5.7 %shard_map.95 = (f32[24,128,128]{2,1,0:T(8,128)S(1)}, bf16[24,128,128]{2,1,0:T(8,128)(2,1)}, bf16[24,128,128]{2,1,0:T(8,128)(2,1)}) custom-call(s32[1,3,12,2]{3,2,1,0:T(8,128)S(1)} %copy.11.pick, bf16[128,1536]{1,0:T(8,128)(2,1)S(1)} %copy-done.4, bf16[1,3,12,2,128,128]{5,4,3,2,1,0:T(8,128)(2,1)S(1)} %copy-done.1), custom_call_target="tpu_custom_call" | custom-call | flops 301989888 | bytes 8388608 | tf_op jit(solution)/shard_map/pallas_call | solution.py:191
  10.9 2.9 %collective-permute-start.4 = (bf16[24,128,128]{2,1,0:T(8,128)(2,1)}, bf16[24,128,128]{2,1,0:T(8,128)(2,1)}, u32[]{:S(2)}, u32[]{:S(2)}) collective-permute-start(bf16[24,128,128]{2,1,0:T(8,128)(2,1)} %get-tuple-element.19), channel_id=1, source_target_pairs={{0,1},{1,0},{2,3},{3,2},{4,5},{5,4},{6,7},{7,6},{8,9},{9,8},{10,11... | collective-permute-start | bytes 2359304 | tf_op jit(solution)/shard_map/ppermute | solution.py:156
  15.9 24.1 %collective-permute-done.rest_1_ = bf16[128,1536]{1,0:T(8,128)(2,1)S(1)} collective-permute-done((bf16[128,1536]{1,0:T(8,128)(2,1)S(1)}, bf16[128,1536]{1,0:T(8,128)(2,1)S(1)}, u32[]{:S(2)}, u32[]{:S(2)}) %collective-permute-start) | collective-permute-done | bytes 393248 | tf_op jit(solution)/shard_map/ppermute | solution.py:156
  41.5 3.5 %shard_map.93 = (f32[24,128,128]{2,1,0:T(8,128)S(1)}, bf16[24,128,128]{2,1,0:T(8,128)(2,1)}) custom-call(s32[1,3,24]{2,1,0:T(4,128)S(1)} %copy.10.pick, bf16[128,1536]{1,0:T(8,128)(2,1)S(1)} %copy-done.2, bf16[128,1536]{1,0:T(8,128)(2,1)S(1)} %collective-permute-done.rest_1_, bf16[128,1536]{1,0:T(8,128)(2,1)S(1)} %collective-permute-done.1.rest_2_, ...), custom_call_target="tpu_custom_call" | custom-call | flops 301989888 | bytes 8388608 | tf_op jit(solution)/shard_map/pallas_call | solution.py:198
  45.4 1.7 collective-permute-start.3
  47.1 9.9 %shard_map.96 = (bf16[3,24,128,128]{3,2,1,0:T(8,128)(2,1)}, f32[12,128,128]{2,1,0:T(8,128)S(1)}, bf16[12,128,128]{2,1,0:T(8,128)(2,1)S(1)}, bf16[12,128,128]{2,1,0:T(8,128)(2,1)S(1)}) custom-call(s32[1,3,24]{2,1,0:T(4,128)S(1)} %copy.10.pick, bf16[128,1536]{1,0:T(8,128)(2,1)S(1)} %copy-done.2, bf16[128,1536]{1,0:T(8,128)(2,1)S(1)} %collective-permute-done.rest_1_, ...), custom_call_target="tpu_custom_call" | custom-call | flops 603979776 | bytes 16777216 | tf_op jit(solution)/shard_map/pallas_call | solution.py:204
  57.0 2.9 %constant_dynamic-slice_fusion.1 = bf16[4608,128]{1,0:T(8,128)(2,1)} fusion(bf16[9216,128]{1,0:T(8,128)(2,1)} %bitcast.6, s32[]{:T(128)S(6)} %select_n.88), kind=kLoop, calls=%fused_computation.29 | loop fusion | bytes 2359300 | tf_op jit(solution)/shard_map/dynamic_slice | solution.py:166
  60.0 1.5 collective-permute-start.6
  63.7 6.0 %shard_map.94 = (bf16[128,1536]{1,0:T(8,128)(2,1)}, bf16[3,12,2,128,128]{4,3,2,1,0:T(8,128)(2,1)S(1)}) custom-call(s32[1,3,12,2]{3,2,1,0:T(8,128)S(1)} %copy-done.9, bf16[24,128,128]{2,1,0:T(8,128)(2,1)} %get-tuple-element.15.rest_0_, bf16[24,128,128]{2,1,0:T(8,128)(2,1)S(1)} %collective-permute-done.2.rest_1_, ...), custom_call_target="tpu_custom_call" | custom-call | flops 603979776 | bytes 12582912 | tf_op jit(solution)/shard_map/pallas_call | solution.py:214
  73.0 1.6 collective-permute-start.9
  74.8 12.4 %collective-permute-done.9 = bf16[2304,128]{1,0:T(8,128)(2,1)S(1)} collective-permute-done((bf16[2304,128]{1,0:T(8,128)(2,1)S(1)}, bf16[2304,128]{1,0:T(8,128)(2,1)S(1)}, u32[]{:S(2)}, u32[]{:S(2)}) %collective-permute-start.9) | collective-permute-done | bytes 589856 | tf_op jit(solution)/shard_map/ppermute | solution.py:156
  88.1 2.5 %collective-permute-start.10 = (bf16[1152,128]{1,0:T(8,128)(2,1)}, bf16[1152,128]{1,0:T(8,128)(2,1)}, u32[]{:S(2)}, u32[]{:S(2)}) collective-permute-start(bf16[1152,128]{1,0:T(8,128)(2,1)} %dynamic-slice_convert_fusion.3), channel_id=1, source_target_pairs={{0,16},{4,20},{8,24},{12,28},{16,0},{20,4},{24,8},{28,12},{1,17},{... | collective-permute-start | bytes 884744 | tf_op jit(solution)/shard_map/ppermute | solution.py:156
  90.8 1.6 collective-permute-start.15
  93.3 9.5 %collective-permute-done.10 = bf16[1152,128]{1,0:T(8,128)(2,1)} collective-permute-done((bf16[1152,128]{1,0:T(8,128)(2,1)}, bf16[1152,128]{1,0:T(8,128)(2,1)}, u32[]{:S(2)}, u32[]{:S(2)}) %collective-permute-start.10) | collective-permute-done | bytes 294944 | tf_op jit(solution)/shard_map/ppermute | solution.py:156
  103.9 9.0 %collective-permute-done.15 = bf16[2304,128]{1,0:T(8,128)(2,1)} collective-permute-done((bf16[2304,128]{1,0:T(8,128)(2,1)S(1)}, bf16[2304,128]{1,0:T(8,128)(2,1)}, u32[]{:S(2)}, u32[]{:S(2)}) %collective-permute-start.15) | collective-permute-done | bytes 589856 | tf_op jit(solution)/shard_map/ppermute | solution.py:156
  114.2 13.1 %collective-permute-done.11 = bf16[1152,128]{1,0:T(8,128)(2,1)S(1)} collective-permute-done((bf16[1152,128]{1,0:T(8,128)(2,1)S(1)}, bf16[1152,128]{1,0:T(8,128)(2,1)S(1)}, u32[]{:S(2)}, u32[]{:S(2)}) %collective-permute-start.11) | collective-permute-done | bytes 294944 | tf_op jit(solution)/shard_map/ppermute | solution.py:156
  127.3 4.3 %collective-permute-done.16 = bf16[1152,128]{1,0:T(8,128)(2,1)S(1)} collective-permute-done((bf16[1152,128]{1,0:T(8,128)(2,1)S(1)}, bf16[1152,128]{1,0:T(8,128)(2,1)S(1)}, u32[]{:S(2)}, u32[]{:S(2)}) %collective-permute-start.16) | collective-permute-done | bytes 294944 | tf_op jit(solution)/shard_map/ppermute | solution.py:156
  131.8 10.7 %collective-permute-start.12 = (bf16[2304,128]{1,0:T(8,128)(2,1)S(1)}, bf16[2304,128]{1,0:T(8,128)(2,1)S(1)}, u32[]{:S(2)}, u32[]{:S(2)}) collective-permute-start(bf16[2304,128]{1,0:T(8,128)(2,1)S(1)} %pad_maximum_fusion.4), channel_id=1, source_target_pairs={{0,8},{4,12},{8,0},{12,4},{16,24},{20,28},{24,16},{28,20},{1,9},{5... | collective-permute-start | bytes 1769480 | tf_op jit(solution)/shard_map/ppermute | solution.py:156
  142.6 7.8 %collective-permute-start.18 = (bf16[2304,128]{1,0:T(8,128)(2,1)S(1)}, bf16[2304,128]{1,0:T(8,128)(2,1)S(1)}, u32[]{:S(2)}, u32[]{:S(2)}) collective-permute-start(bf16[2304,128]{1,0:T(8,128)(2,1)S(1)} %pad_maximum_fusion.5), channel_id=1, source_target_pairs={{0,8},{4,12},{8,0},{12,4},{16,24},{20,28},{24,16},{28,20},{1,9},{5... | collective-permute-start | bytes 1769480 | tf_op jit(solution)/shard_map/ppermute | solution.py:156
  150.5 6.3 %collective-permute-done.12 = bf16[2304,128]{1,0:T(8,128)(2,1)S(1)} collective-permute-done((bf16[2304,128]{1,0:T(8,128)(2,1)S(1)}, bf16[2304,128]{1,0:T(8,128)(2,1)S(1)}, u32[]{:S(2)}, u32[]{:S(2)}) %collective-permute-start.12) | collective-permute-done | bytes 589856 | tf_op jit(solution)/shard_map/ppermute | solution.py:156
  157.2 10.8 %collective-permute-done.18 = bf16[2304,128]{1,0:T(8,128)(2,1)S(1)} collective-permute-done((bf16[2304,128]{1,0:T(8,128)(2,1)S(1)}, bf16[2304,128]{1,0:T(8,128)(2,1)S(1)}, u32[]{:S(2)}, u32[]{:S(2)}) %collective-permute-start.18) | collective-permute-done | bytes 589856 | tf_op jit(solution)/shard_map/ppermute | solution.py:156
  168.9 9.3 %pad_maximum_fusion = bf16[9216,128]{1,0:T(8,128)(2,1)} fusion(bf16[4608,128]{1,0:T(8,128)(2,1)S(1)} %get-tuple-element.29, bf16[4608,128]{1,0:T(8,128)(2,1)S(1)} %get-tuple-element.28), kind=kLoop, calls=%fused_computation | loop fusion | flops 4718592 | bytes 4718592 | tf_op jit(solution)/shard_map/concatenate | solution.py:175
  178.6 9.4 %pad_maximum_fusion.1 = bf16[9216,128]{1,0:T(8,128)(2,1)} fusion(bf16[4608,128]{1,0:T(8,128)(2,1)S(1)} %get-tuple-element.27, bf16[4608,128]{1,0:T(8,128)(2,1)S(1)} %get-tuple-element.26), kind=kLoop, calls=%fused_computation.1 | loop fusion | flops 4718592 | bytes 4718592 | tf_op jit(solution)/shard_map/concatenate | solution.py:175
  (79 shorter events, 18.7 us)
Async XLA Ops:
  4.1 11.8 %copy-start.15 = (s32[1,3,24]{2,0,1:T(1,128)S(1)}, s32[1,3,24]{2,0,1:T(1,128)}, u32[]{:S(2)}) copy-start(s32[1,3,24]{2,0,1:T(1,128)} %param.8) | copy-start | bytes 868
  4.1 37.4 %copy-start = (bf16[1,3,24,128,128]{4,3,2,1,0:T(8,128)(2,1)S(1)}, bf16[1,3,24,128,128]{4,3,2,1,0:T(8,128)(2,1)}, u32[]{:S(2)}) copy-start(bf16[1,3,24,128,128]{4,3,2,1,0:T(8,128)(2,1)} %rest_3_.5) | copy-start | bytes 7077892
  10.9 36.2 %collective-permute-start.4 = (bf16[24,128,128]{2,1,0:T(8,128)(2,1)}, bf16[24,128,128]{2,1,0:T(8,128)(2,1)}, u32[]{:S(2)}, u32[]{:S(2)}) collective-permute-start(bf16[24,128,128]{2,1,0:T(8,128)(2,1)} %get-tuple-element.19), channel_id=1, source_target_pairs={{0,1},{1,0},{2,3},{3,2},{4,5},{5,4},{6,7},{7,6},{8,9},{9,8},{10,11... | collective-permute-start | bytes 2359304 | tf_op jit(solution)/shard_map/ppermute | solution.py:156
  13.8 33.3 %collective-permute-start.5 = (bf16[24,128,128]{2,1,0:T(8,128)(2,1)}, bf16[24,128,128]{2,1,0:T(8,128)(2,1)}, u32[]{:S(2)}, u32[]{:S(2)}) collective-permute-start(bf16[24,128,128]{2,1,0:T(8,128)(2,1)} %get-tuple-element.20), channel_id=1, source_target_pairs={{0,2},{1,3},{2,0},{3,1},{4,6},{5,7},{6,4},{7,5},{8,10},{9,11},{10,... | collective-permute-start | bytes 2359304 | tf_op jit(solution)/shard_map/ppermute | solution.py:156
  15.4 24.7 %collective-permute-start = (bf16[128,1536]{1,0:T(8,128)(2,1)S(1)}, bf16[128,1536]{1,0:T(8,128)(2,1)S(1)}, u32[]{:S(2)}, u32[]{:S(2)}) collective-permute-start(bf16[128,1536]{1,0:T(8,128)(2,1)S(1)} %copy-done.2), channel_id=1, source_target_pairs={{0,1},{1,0},{2,3},{3,2},{4,5},{5,4},{6,7},{7,6},{8,9},{9,8},{10,11... | collective-permute-start | bytes 1179656 | tf_op jit(solution)/shard_map/ppermute | solution.py:156
  15.9 25.6 %collective-permute-start.1 = (bf16[128,1536]{1,0:T(8,128)(2,1)S(1)}, bf16[128,1536]{1,0:T(8,128)(2,1)S(1)}, u32[]{:S(2)}, u32[]{:S(2)}) collective-permute-start(bf16[128,1536]{1,0:T(8,128)(2,1)S(1)} %copy-done.2), channel_id=1, source_target_pairs={{0,2},{1,3},{2,0},{3,1},{4,6},{5,7},{6,4},{7,5},{8,10},{9,11},{10,... | collective-permute-start | bytes 1179656 | tf_op jit(solution)/shard_map/ppermute | solution.py:156
  45.0 18.3 %collective-permute-start.2 = (bf16[24,128,128]{2,1,0:T(8,128)(2,1)}, bf16[24,128,128]{2,1,0:T(8,128)(2,1)S(1)}, u32[]{:S(2)}, u32[]{:S(2)}) collective-permute-start(bf16[24,128,128]{2,1,0:T(8,128)(2,1)} %get-tuple-element.15.rest_0_), channel_id=1, source_target_pairs={{0,1},{1,0},{2,3},{3,2},{4,5},{5,4},{6,7},{7,6},{8,9},{9,8},{10,11... | collective-permute-start | bytes 2359304 | tf_op jit(solution)/shard_map/ppermute | solution.py:156
  45.4 18.3 %collective-permute-start.3 = (bf16[24,128,128]{2,1,0:T(8,128)(2,1)}, bf16[24,128,128]{2,1,0:T(8,128)(2,1)S(1)}, u32[]{:S(2)}, u32[]{:S(2)}) collective-permute-start(bf16[24,128,128]{2,1,0:T(8,128)(2,1)} %get-tuple-element.15.rest_0_), channel_id=1, source_target_pairs={{0,2},{1,3},{2,0},{3,1},{4,6},{5,7},{6,4},{7,5},{8,10},{9,11},{10,... | collective-permute-start | bytes 2359304 | tf_op jit(solution)/shard_map/ppermute | solution.py:156
  60.0 9.9 %collective-permute-start.8 = (bf16[4608,128]{1,0:T(8,128)(2,1)}, bf16[4608,128]{1,0:T(8,128)(2,1)}, u32[]{:S(2)}, u32[]{:S(2)}) collective-permute-start(bf16[4608,128]{1,0:T(8,128)(2,1)} %constant_dynamic-slice_fusion.1), channel_id=1, source_target_pairs={{0,4},{4,0},{8,12},{12,8},{16,20},{20,16},{24,28},{28,24},{1,5},{5... | collective-permute-start | bytes 3538952 | tf_op jit(solution)/shard_map/ppermute | solution.py:156
  60.0 32.3 %collective-permute-start.6 = (bf16[12,128,128]{2,1,0:T(8,128)(2,1)}, bf16[12,128,128]{2,1,0:T(8,128)(2,1)S(1)}, u32[]{:S(2)}, u32[]{:S(2)}) collective-permute-start(bf16[12,128,128]{2,1,0:T(8,128)(2,1)} %copy-done.11), channel_id=1, source_target_pairs={{0,1},{1,0},{2,3},{3,2},{4,5},{5,4},{6,7},{7,6},{8,9},{9,8},{10,11... | collective-permute-start | bytes 1179656 | tf_op jit(solution)/shard_map/ppermute | solution.py:156
  61.6 30.8 %collective-permute-start.7 = (bf16[12,128,128]{2,1,0:T(8,128)(2,1)}, bf16[12,128,128]{2,1,0:T(8,128)(2,1)S(1)}, u32[]{:S(2)}, u32[]{:S(2)}) collective-permute-start(bf16[12,128,128]{2,1,0:T(8,128)(2,1)} %copy-done.10), channel_id=1, source_target_pairs={{0,2},{1,3},{2,0},{3,1},{4,6},{5,7},{6,4},{7,5},{8,10},{9,11},{10,... | collective-permute-start | bytes 1179656 | tf_op jit(solution)/shard_map/ppermute | solution.py:156
  69.8 4.8 %collective-permute-start.14 = (bf16[4608,128]{1,0:T(8,128)(2,1)S(1)}, bf16[4608,128]{1,0:T(8,128)(2,1)S(1)}, u32[]{:S(2)}, u32[]{:S(2)}) collective-permute-start(bf16[4608,128]{1,0:T(8,128)(2,1)S(1)} %constant_dynamic-slice_fusion), channel_id=1, source_target_pairs={{0,4},{4,0},{8,12},{12,8},{16,20},{20,16},{24,28},{28,24},{1,5},{5... | collective-permute-start | bytes 3538952 | tf_op jit(solution)/shard_map/ppermute | solution.py:156
  73.0 14.3 %collective-permute-start.9 = (bf16[2304,128]{1,0:T(8,128)(2,1)S(1)}, bf16[2304,128]{1,0:T(8,128)(2,1)S(1)}, u32[]{:S(2)}, u32[]{:S(2)}) collective-permute-start(bf16[2304,128]{1,0:T(8,128)(2,1)S(1)} %dynamic-slice_convert_fusion.1), channel_id=1, source_target_pairs={{0,8},{4,12},{8,0},{12,4},{16,24},{20,28},{24,16},{28,20},{1,9},{5... | collective-permute-start | bytes 1769480 | tf_op jit(solution)/shard_map/ppermute | solution.py:156
  74.8 15.9 %copy-start.12 = (f32[4608,128]{1,0:T(8,128)}, f32[4608,128]{1,0:T(8,128)S(1)}, u32[]{:S(2)}) copy-start(f32[4608,128]{1,0:T(8,128)S(1)} %convert_add_fusion) | copy-start | bytes 7077892
  88.1 14.6 %collective-permute-start.10 = (bf16[1152,128]{1,0:T(8,128)(2,1)}, bf16[1152,128]{1,0:T(8,128)(2,1)}, u32[]{:S(2)}, u32[]{:S(2)}) collective-permute-start(bf16[1152,128]{1,0:T(8,128)(2,1)} %dynamic-slice_convert_fusion.3), channel_id=1, source_target_pairs={{0,16},{4,20},{8,24},{12,28},{16,0},{20,4},{24,8},{28,12},{1,17},{... | collective-permute-start | bytes 884744 | tf_op jit(solution)/shard_map/ppermute | solution.py:156
  90.8 22.1 %collective-permute-start.15 = (bf16[2304,128]{1,0:T(8,128)(2,1)S(1)}, bf16[2304,128]{1,0:T(8,128)(2,1)}, u32[]{:S(2)}, u32[]{:S(2)}) collective-permute-start(bf16[2304,128]{1,0:T(8,128)(2,1)S(1)} %dynamic-slice_convert_fusion), channel_id=1, source_target_pairs={{0,8},{4,12},{8,0},{12,4},{16,24},{20,28},{24,16},{28,20},{1,9},{5... | collective-permute-start | bytes 1769480 | tf_op jit(solution)/shard_map/ppermute | solution.py:156
  92.4 20.5 %copy-start.13 = (f32[4608,128]{1,0:T(8,128)S(1)}, f32[4608,128]{1,0:T(8,128)}, u32[]{:S(2)}) copy-start(f32[4608,128]{1,0:T(8,128)} %copy-done.12) | copy-start | bytes 7077892
  103.8 23.5 %collective-permute-start.11 = (bf16[1152,128]{1,0:T(8,128)(2,1)S(1)}, bf16[1152,128]{1,0:T(8,128)(2,1)S(1)}, u32[]{:S(2)}, u32[]{:S(2)}) collective-permute-start(bf16[1152,128]{1,0:T(8,128)(2,1)S(1)} %multiply_convert_fusion.1), channel_id=1, source_target_pairs={{0,16},{4,20},{8,24},{12,28},{16,0},{20,4},{24,8},{28,12},{1,17},{... | collective-permute-start | bytes 884744 | tf_op jit(solution)/shard_map/ppermute | solution.py:156
  114.1 17.5 %collective-permute-start.16 = (bf16[1152,128]{1,0:T(8,128)(2,1)S(1)}, bf16[1152,128]{1,0:T(8,128)(2,1)S(1)}, u32[]{:S(2)}, u32[]{:S(2)}) collective-permute-start(bf16[1152,128]{1,0:T(8,128)(2,1)S(1)} %dynamic-slice_convert_fusion.2), channel_id=1, source_target_pairs={{0,16},{4,20},{8,24},{12,28},{16,0},{20,4},{24,8},{28,12},{1,17},{... | collective-permute-start | bytes 884744 | tf_op jit(solution)/shard_map/ppermute | solution.py:156
  131.7 10.9 %collective-permute-start.17 = (bf16[1152,128]{1,0:T(8,128)(2,1)S(1)}, bf16[1152,128]{1,0:T(8,128)(2,1)S(1)}, u32[]{:S(2)}, u32[]{:S(2)}) collective-permute-start(bf16[1152,128]{1,0:T(8,128)(2,1)S(1)} %multiply_convert_fusion), channel_id=1, source_target_pairs={{0,16},{4,20},{8,24},{12,28},{16,0},{20,4},{24,8},{28,12},{1,17},{... | collective-permute-start | bytes 884744 | tf_op jit(solution)/shard_map/ppermute | solution.py:156
  131.8 24.9 %collective-permute-start.12 = (bf16[2304,128]{1,0:T(8,128)(2,1)S(1)}, bf16[2304,128]{1,0:T(8,128)(2,1)S(1)}, u32[]{:S(2)}, u32[]{:S(2)}) collective-permute-start(bf16[2304,128]{1,0:T(8,128)(2,1)S(1)} %pad_maximum_fusion.4), channel_id=1, source_target_pairs={{0,8},{4,12},{8,0},{12,4},{16,24},{20,28},{24,16},{28,20},{1,9},{5... | collective-permute-start | bytes 1769480 | tf_op jit(solution)/shard_map/ppermute | solution.py:156
  142.6 25.4 %collective-permute-start.18 = (bf16[2304,128]{1,0:T(8,128)(2,1)S(1)}, bf16[2304,128]{1,0:T(8,128)(2,1)S(1)}, u32[]{:S(2)}, u32[]{:S(2)}) collective-permute-start(bf16[2304,128]{1,0:T(8,128)(2,1)S(1)} %pad_maximum_fusion.5), channel_id=1, source_target_pairs={{0,8},{4,12},{8,0},{12,4},{16,24},{20,28},{24,16},{28,20},{1,9},{5... | collective-permute-start | bytes 1769480 | tf_op jit(solution)/shard_map/ppermute | solution.py:156
  157.1 11.3 %collective-permute-start.13 = (bf16[4608,128]{1,0:T(8,128)(2,1)S(1)}, bf16[4608,128]{1,0:T(8,128)(2,1)S(1)}, u32[]{:S(2)}, u32[]{:S(2)}) collective-permute-start(bf16[4608,128]{1,0:T(8,128)(2,1)S(1)} %pad_maximum_fusion.2), channel_id=1, source_target_pairs={{0,4},{4,0},{8,12},{12,8},{16,20},{20,16},{24,28},{28,24},{1,5},{5... | collective-permute-start | bytes 3538952 | tf_op jit(solution)/shard_map/ppermute | solution.py:156
  168.3 9.8 %collective-permute-start.19 = (bf16[4608,128]{1,0:T(8,128)(2,1)S(1)}, bf16[4608,128]{1,0:T(8,128)(2,1)S(1)}, u32[]{:S(2)}, u32[]{:S(2)}) collective-permute-start(bf16[4608,128]{1,0:T(8,128)(2,1)S(1)} %pad_maximum_fusion.3), channel_id=1, source_target_pairs={{0,4},{4,0},{8,12},{12,8},{16,20},{20,16},{24,28},{28,24},{1,5},{5... | collective-permute-start | bytes 3538952 | tf_op jit(solution)/shard_map/ppermute | solution.py:156
  (12 other events, 49.8 us)

commit v2 on v1

--- a/solution.py
+++ b/solution.py
@@ -174,6 +174,123 @@
         last = jnp.where(mine == 0, other, value)
         value = jnp.concatenate([first, last], axis=0)
     return value.reshape((1,) + part.shape)
+
+
+def stream_count(rows, devices):
+    return next((n for n in (4, 2, 1) if rows % (16 * devices * n) == 0), 0)
+
+
+def sum_streams_body(count, streams, bits, scale, *refs):
+    parts, outs = refs[:count], refs[count : 2 * count]
+    acc, stage, land, send_sem, recv_sem = refs[2 * count :]
+    me = lax.axis_index("dp")
+    mine = [lax.rem(lax.div(me, 1 << b), 2) for b in range(bits)]
+    peer = [me + (1 - 2 * mine[b]) * (1 << b) for b in range(bits)]
+    rows = parts[0].shape[0] // streams
+    size = [rows >> (b + 1) for b in range(bits)]
+    total = count * streams
+
+    barrier = pltpu.get_barrier_semaphore()
+    for b in range(bits):
+        pl.semaphore_signal(
+            barrier, inc=1, device_id={"dp": peer[b]}, device_id_type=pl.DeviceIdType.MESH
+        )
+    pl.semaphore_wait(barrier, bits)
+
+    start = [0] * (bits + 1)
+    for b in range(bits):
+        start[b + 1] = start[b] + mine[b] * size[b]
+    place = [0]
+    for b in range(bits):
+        place.append(place[b] + size[b])
+
+    def span(at, length):
+        return pl.ds(pl.multiple_of(at, 16), length)
+
+    def copy(j, step):
+        which, base = j // streams, (j % streams) * rows
+        if step < bits:
+            b = step
+            there = start[b] + (1 - mine[b]) * size[b]
+            source = (
+                parts[which].at[span(base + there, size[0])]
+                if b == 0
+                else stage.at[j, pl.ds(place[b] - size[0], size[b])]
+            )
+            target = land.at[j, pl.ds(place[b], size[b])]
+        else:
+            b = 2 * bits - 1 - step
+            source = target = outs[which].at[span(base + start[b + 1], size[b])]
+        return pltpu.make_async_remote_copy(
+            src_ref=source,
+            dst_ref=target,
+            send_sem=send_sem.at[j, step],
+            recv_sem=recv_sem.at[j, step],
+            device_id={"dp": peer[b]},
+            device_id_type=pl.DeviceIdType.MESH,
+        )
+
+    def advance(j, step):
+        which, base = j // streams, (j % streams) * rows
+        if step > 0:
+            copy(j, step - 1).wait_recv()
+        if 0 < step <= bits:
+            b = step - 1
+            arrived = land[j, pl.ds(place[b], size[b])].astype(jnp.float32)
+            if b == 0:
+                held = parts[which][span(base + mine[0] * size[0], size[0])].astype(jnp.float32)
+            else:
+                held = acc[j, span(start[b + 1] - start[1], size[b])]
+            value = held + arrived
+            if step == bits:
+                outs[which][span(base + start[bits], size[b])] = (value * scale).astype(jnp.bfloat16)
+            else:
+                acc[j, span(start[b + 1] - start[1], size[b])] = value
+                away = start[step] - start[1] + (1 - mine[step]) * size[step]
+                stage[j, pl.ds(place[step] - size[0], size[step])] = acc[
+                    j, span(away, size[step])
+                ].astype(jnp.bfloat16)
+        if step < 2 * bits:
+            copy(j, step).start()
+
+    for tick in range(2 * bits + total):
+        for j in range(total):
+            if 0 <= tick - j <= 2 * bits:
+                advance(j, tick - j)
+    for j in range(total):
+        for step in range(2 * bits):
+            copy(j, step).wait_send()
+
+
+def token_sums(parts, scale):
+    devices = lax.axis_size("dp")
+    bits = devices.bit_length() - 1
+    flat = [p.reshape(-1, p.shape[-1]) for p in parts]
+    height, width = flat[0].shape
+    streams = stream_count(height, devices)
+    if not streams or bits < 2 or any(f.shape != flat[0].shape for f in flat):
+        return [token_sum(p, scale) for p in parts]
+    count, rows = len(parts), height // streams
+    total = count * streams
+    moved = [rows >> (b + 1) for b in range(bits)]
+    sums = pl.pallas_call(
+        functools.partial(sum_streams_body, count, streams, bits, scale),
+        out_shape=[jax.ShapeDtypeStruct(f.shape, BF16) for f in flat],
+        in_specs=[VM] * count,
+        out_specs=[VM] * count,
+        scratch_shapes=[
+            pltpu.VMEM((total, moved[0], width), F32),
+            pltpu.VMEM((total, sum(moved[1:]), width), BF16),
+            pltpu.VMEM((total, sum(moved), width), BF16),
+            pltpu.SemaphoreType.DMA((total, 2 * bits)),
+            pltpu.SemaphoreType.DMA((total, 2 * bits)),
+        ],
+        compiler_params=pltpu.CompilerParams(
+            collective_id=0, has_side_effects=True, vmem_limit_bytes=48 * 2**20
+        ),
+        cost_estimate=pl.CostEstimate(flops=2**20, bytes_accessed=200 * 2**20, transcendentals=0),
+    )(*flat)
+    return [s.reshape((1,) + p.shape) for s, p in zip(sums, parts)]
 
 
 def local(inputs, up_weight, up_pick, down_weight, down_pick, cotangent):
@@ -217,8 +334,7 @@
         2 * macs, 12 * 2**20, [SM] + [VM] * (levels + 2),
     )(down_pick, *acts, down_weight, cotangent)
     backs = [back[0]] + [swap(back[b + 1], "mp", b) for b in range(bit_count)]
-    up_out = token_sum(up_part, scale)
-    down_out = token_sum(down_part, scale)
+    up_out, down_out = token_sums([up_part, down_part], scale)
     [grad_inputs] = call(
         functools.partial(sum_body, levels),
         [((tokens, width), BF16)], 2**20, 2 * 2**20, [VM] * levels,

time: 192 us -> 155 us (0.81); the launches traced: 188 us -> 155 us
  Pallas kernels: 26 us -> 115 us
  waiting for transfers between devices: 92.6 us -> 19.6 us
  other arithmetic: 24.5 us -> 0 us
  starting transfers between devices: 34 us -> 10.6 us
    pallas_call x0 -> x1, Pallas kernels: none -> 91.8 us  [token_sums(): pl.pallas_call(functools.partial(sum_streams_body, count, streams, bits,...]
    ppermute x20 -> x8, waiting for transfers between devices: 92.6 us -> 19.6 us  [swap(): return lax.ppermute(block, axis, [(i, i ^ 1 << bit) for i in range(count)])]
    ppermute x20 -> x8, starting transfers between devices: 34 us -> 10.6 us  [swap(): return lax.ppermute(block, axis, [(i, i ^ 1 << bit) for i in range(count)])]
    concatenate x6 -> x0, other arithmetic: 18.9 us -> none  [token_sum(): value = jnp.concatenate([first, last], axis=0)]
    dynamic_slice x2 -> x0, local copies, waits for them, and re-layouts: 3.02 us -> none  [token_sum(): sent = lax.dynamic_slice_in_dim(value, (1 - mine) * rows, rows).astype(BF16)]
    add x4 -> x0, other arithmetic: 2.99 us -> none  [token_sum(): value = kept + swap(sent, 'dp', bit).astype(F32)]
    unnamed x34 -> x20, local copies, waits for them, and re-layouts: 6.14 us -> 8.81 us
  transfers between devices with their start and end apart: 20 -> 8, of which waited for: 11 -> 4; matrix products, arithmetic and copies ran while one was open for 10% -> 1% of each run, Pallas kernels for 11% -> 74%
where the time goes in v2:
time: 155 us
  Pallas kernels  115 us (74%)
  waiting for transfers between devices  19.6 us (13%)
  starting transfers between devices  10.6 us (7%)
  local copies, waits for them, and re-layouts  8.81 us (6%)
    pallas_call x1, Pallas kernels, token_sums(): pl.pallas_call(functools.partial(sum_streams_body, count, streams, bits,...  91.8 us
    ppermute x8, waiting for transfers between devices, swap(): return lax.ppermute(block, axis, [(i, i ^ 1 << bit) for i in range(count)])  19.6 us
    ppermute x8, starting transfers between devices, swap(): return lax.ppermute(block, axis, [(i, i ^ 1 << bit) for i in range(count)])  10.6 us
    pallas_call x1, Pallas kernels, local(): call(functools.partial(mid_body, levels), [((levels, hid_blocks, size, si...  9.48 us
    unnamed x20, local copies, waits for them, and re-layouts  8.81 us
    pallas_call x1, Pallas kernels, local(): call(functools.partial(down_body, levels), [((tokens, width), BF16), ((le...  5.8 us
    pallas_call x1, Pallas kernels, local(): call(functools.partial(back_body, levels), [(hid, F32)] + [(hid, BF16)] *...  4.68 us
  transfers between devices with their start and end apart: 8, of which 4 were waited for; matrix products, arithmetic and copies ran while one was open for 1% of the time, Pallas kernels for 74%

profile of v2, /device:TPU:0, one launch (start us, length us, event | category | flops | bytes accessed | tf_op | source)
XLA Modules:
  0.0 155.0 jit_solution(17513193470233232564)
XLA Ops:
  0.6 3.0 %collective-permute-start = (bf16[128,1536]{1,0:T(8,128)(2,1)}, bf16[128,1536]{1,0:T(8,128)(2,1)S(1)}, u32[]{:S(2)}, u32[]{:S(2)}) collective-permute-start(bf16[128,1536]{1,0:T(8,128)(2,1)} %rest_0_.3), channel_id=1, source_target_pairs={{0,1},{1,0},{2,3},{3,2},{4,5},{5,4},{6,7},{7,6},{8,9},{9,8},{10,11... | collective-permute-start | bytes 1179656 | tf_op jit(solution)/shard_map/ppermute | solution.py:156
  3.6 1.5 collective-permute-start.1
  5.2 0.8 copy.11.pick
  6.0 1.7 %copy-done.1 = bf16[1,3,12,2,128,128]{5,4,3,2,1,0:T(8,128)(2,1)S(1)} copy-done((bf16[1,3,12,2,128,128]{5,4,3,2,1,0:T(8,128)(2,1)S(1)}, bf16[1,3,12,2,128,128]{5,4,3,2,1,0:T(8,128)(2,1)}, u32[]{:S(2)}) %copy-start.1) | copy-done | bytes 2359320
  7.6 1.0 copy-done.5
  8.6 4.7 %shard_map.95 = (f32[24,128,128]{2,1,0:T(8,128)S(1)}, bf16[24,128,128]{2,1,0:T(8,128)(2,1)S(1)}, bf16[24,128,128]{2,1,0:T(8,128)(2,1)S(1)}) custom-call(s32[1,3,12,2]{3,2,1,0:T(8,128)S(1)} %copy.11.pick, bf16[128,1536]{1,0:T(8,128)(2,1)S(1)} %copy-done.5, bf16[1,3,12,2,128,128]{5,4,3,2,1,0:T(8,128)(2,1)S(1)} %copy-done.1), custom_call_target="tpu_custom_call" | custom-call | flops 301989888 | bytes 8388608 | tf_op jit(solution)/shard_map/pallas_call | solution.py:308
  13.3 1.1 copy-done.4
  14.4 0.5 collective-permute-start.4
  15.1 2.7 %shard_map.93 = (f32[24,128,128]{2,1,0:T(8,128)S(1)}, bf16[24,128,128]{2,1,0:T(8,128)(2,1)S(1)}) custom-call(s32[1,3,24]{2,1,0:T(4,128)S(1)} %copy.10.pick, bf16[128,1536]{1,0:T(8,128)(2,1)S(1)} %copy-done.3, bf16[128,1536]{1,0:T(8,128)(2,1)S(1)} %collective-permute-done.rest_1_, bf16[128,1536]{1,0:T(8,128)(2,1)S(1)} %collective-permute-done.1.rest_2_, ...), custom_call_target="tpu_custom_call" | custom-call | flops 301989888 | bytes 8388608 | tf_op jit(solution)/shard_map/pallas_call | solution.py:315
  17.8 2.0 %collective-permute-start.2 = (bf16[24,128,128]{2,1,0:T(8,128)(2,1)S(1)}, bf16[24,128,128]{2,1,0:T(8,128)(2,1)S(1)}, u32[]{:S(2)}, u32[]{:S(2)}) collective-permute-start(bf16[24,128,128]{2,1,0:T(8,128)(2,1)S(1)} %get-tuple-element.17.rest_0_), channel_id=1, source_target_pairs={{0,1},{1,0},{2,3},{3,2},{4,5},{5,4},{6,7},{7,6},{8,9},{9,8},{10,11... | collective-permute-start | bytes 2359304 | tf_op jit(solution)/shard_map/ppermute | solution.py:156
  19.8 1.5 collective-permute-start.3
  21.3 13.7 %collective-permute-done.4.rest_6_ = bf16[24,128,128]{2,1,0:T(8,128)(2,1)S(1)} collective-permute-done((bf16[24,128,128]{2,1,0:T(8,128)(2,1)S(1)}, bf16[24,128,128]{2,1,0:T(8,128)(2,1)S(1)}, u32[]{:S(2)}, u32[]{:S(2)}) %collective-permute-start.4) | collective-permute-done | bytes 786464 | tf_op jit(solution)/shard_map/ppermute | solution.py:156
  34.9 0.5 collective-permute-done.5.rest_7_
  35.5 9.5 %shard_map.96 = (bf16[3,24,128,128]{3,2,1,0:T(8,128)(2,1)}, f32[12,128,128]{2,1,0:T(8,128)S(1)}, bf16[12,128,128]{2,1,0:T(8,128)(2,1)S(1)}, bf16[12,128,128]{2,1,0:T(8,128)(2,1)S(1)}) custom-call(s32[1,3,24]{2,1,0:T(4,128)S(1)} %copy.10.pick, bf16[128,1536]{1,0:T(8,128)(2,1)S(1)} %copy-done.3, bf16[128,1536]{1,0:T(8,128)(2,1)S(1)} %collective-permute-done.rest_1_, ...), custom_call_target="tpu_custom_call" | custom-call | flops 603979776 | bytes 16777216 | tf_op jit(solution)/shard_map/pallas_call | solution.py:321
  44.9 1.4 collective-permute-start.6
  46.4 0.5 collective-permute-start.7
  46.9 4.9 %collective-permute-done.2.rest_1_ = bf16[24,128,128]{2,1,0:T(8,128)(2,1)S(1)} collective-permute-done((bf16[24,128,128]{2,1,0:T(8,128)(2,1)S(1)}, bf16[24,128,128]{2,1,0:T(8,128)(2,1)S(1)}, u32[]{:S(2)}, u32[]{:S(2)}) %collective-permute-start.2) | collective-permute-done | bytes 786464 | tf_op jit(solution)/shard_map/ppermute | solution.py:156
  51.8 0.5 collective-permute-done.3.rest_2_
  52.3 5.8 %shard_map.94 = (bf16[128,1536]{1,0:T(8,128)(2,1)}, bf16[3,12,2,128,128]{4,3,2,1,0:T(8,128)(2,1)S(1)}) custom-call(s32[1,3,12,2]{3,2,1,0:T(8,128)S(1)} %copy.11.pick, bf16[24,128,128]{2,1,0:T(8,128)(2,1)S(1)} %get-tuple-element.17.rest_0_, bf16[24,128,128]{2,1,0:T(8,128)(2,1)S(1)} %collective-permute-done.2.rest_1_, ...), custom_call_target="tpu_custom_call" | custom-call | flops 603979776 | bytes 12582912 | tf_op jit(solution)/shard_map/pallas_call | solution.py:331
  58.1 1.4 copy-done.2
  59.5 91.8 %shard_map.98 = (bf16[9216,128]{1,0:T(8,128)(2,1)S(1)}, bf16[9216,128]{1,0:T(8,128)(2,1)S(1)}) custom-call(bf16[9216,128]{1,0:T(8,128)(2,1)} %bitcast.7, bf16[9216,128]{1,0:T(8,128)(2,1)} %bitcast.6), custom_call_target="tpu_custom_call" | custom-call | flops 1048576 | bytes 209715200 | tf_op jit(solution)/shard_map/pallas_call | solution.py:276
  151.3 0.9 shard_map.97
  152.2 1.4 copy.16
  153.6 1.4 copy.17
  (18 shorter events, 0.1 us)
Async XLA Ops:
  0.6 14.5 %copy-start = (bf16[1,3,24,128,128]{4,3,2,1,0:T(8,128)(2,1)S(1)}, bf16[1,3,24,128,128]{4,3,2,1,0:T(8,128)(2,1)}, u32[]{:S(2)}) copy-start(bf16[1,3,24,128,128]{4,3,2,1,0:T(8,128)(2,1)} %rest_3_.5) | copy-start | bytes 7077892
  0.6 14.4 %collective-permute-start = (bf16[128,1536]{1,0:T(8,128)(2,1)}, bf16[128,1536]{1,0:T(8,128)(2,1)S(1)}, u32[]{:S(2)}, u32[]{:S(2)}) collective-permute-start(bf16[128,1536]{1,0:T(8,128)(2,1)} %rest_0_.3), channel_id=1, source_target_pairs={{0,1},{1,0},{2,3},{3,2},{4,5},{5,4},{6,7},{7,6},{8,9},{9,8},{10,11... | collective-permute-start | bytes 1179656 | tf_op jit(solution)/shard_map/ppermute | solution.py:156
  3.6 11.4 %collective-permute-start.1 = (bf16[128,1536]{1,0:T(8,128)(2,1)}, bf16[128,1536]{1,0:T(8,128)(2,1)S(1)}, u32[]{:S(2)}, u32[]{:S(2)}) collective-permute-start(bf16[128,1536]{1,0:T(8,128)(2,1)} %rest_0_.3), channel_id=1, source_target_pairs={{0,2},{1,3},{2,0},{3,1},{4,6},{5,7},{6,4},{7,5},{8,10},{9,11},{10,... | collective-permute-start | bytes 1179656 | tf_op jit(solution)/shard_map/ppermute | solution.py:156
  6.0 1.7 %copy-start.1 = (bf16[1,3,12,2,128,128]{5,4,3,2,1,0:T(8,128)(2,1)S(1)}, bf16[1,3,12,2,128,128]{5,4,3,2,1,0:T(8,128)(2,1)}, u32[]{:S(2)}) copy-start(bf16[1,3,12,2,128,128]{5,4,3,2,1,0:T(8,128)(2,1)} %weight.1) | copy-start | bytes 7077892
  7.6 1.0 copy-start.5
  8.6 6.5 %copy-start.7 = (s32[1,3,24]{2,0,1:T(1,128)S(1)}, s32[1,3,24]{2,0,1:T(1,128)}, u32[]{:S(2)}) copy-start(s32[1,3,24]{2,0,1:T(1,128)} %param.8) | copy-start | bytes 868
  8.6 6.5 %copy-start.3 = (bf16[128,1536]{1,0:T(8,128)(2,1)S(1)}, bf16[128,1536]{1,0:T(8,128)(2,1)}, u32[]{:S(2)}) copy-start(bf16[128,1536]{1,0:T(8,128)(2,1)} %rest_0_.3) | copy-start | bytes 1179652
  13.3 1.1 copy-start.4
  14.4 20.5 %collective-permute-start.4 = (bf16[24,128,128]{2,1,0:T(8,128)(2,1)S(1)}, bf16[24,128,128]{2,1,0:T(8,128)(2,1)S(1)}, u32[]{:S(2)}, u32[]{:S(2)}) collective-permute-start(bf16[24,128,128]{2,1,0:T(8,128)(2,1)S(1)} %get-tuple-element.21), channel_id=1, source_target_pairs={{0,1},{1,0},{2,3},{3,2},{4,5},{5,4},{6,7},{7,6},{8,9},{9,8},{10,11... | collective-permute-start | bytes 2359304 | tf_op jit(solution)/shard_map/ppermute | solution.py:156
  15.0 20.5 %collective-permute-start.5 = (bf16[24,128,128]{2,1,0:T(8,128)(2,1)S(1)}, bf16[24,128,128]{2,1,0:T(8,128)(2,1)S(1)}, u32[]{:S(2)}, u32[]{:S(2)}) collective-permute-start(bf16[24,128,128]{2,1,0:T(8,128)(2,1)S(1)} %get-tuple-element.22), channel_id=1, source_target_pairs={{0,2},{1,3},{2,0},{3,1},{4,6},{5,7},{6,4},{7,5},{8,10},{9,11},{10,... | collective-permute-start | bytes 2359304 | tf_op jit(solution)/shard_map/ppermute | solution.py:156
  17.8 34.0 %collective-permute-start.2 = (bf16[24,128,128]{2,1,0:T(8,128)(2,1)S(1)}, bf16[24,128,128]{2,1,0:T(8,128)(2,1)S(1)}, u32[]{:S(2)}, u32[]{:S(2)}) collective-permute-start(bf16[24,128,128]{2,1,0:T(8,128)(2,1)S(1)} %get-tuple-element.17.rest_0_), channel_id=1, source_target_pairs={{0,1},{1,0},{2,3},{3,2},{4,5},{5,4},{6,7},{7,6},{8,9},{9,8},{10,11... | collective-permute-start | bytes 2359304 | tf_op jit(solution)/shard_map/ppermute | solution.py:156
  19.8 32.6 %collective-permute-start.3 = (bf16[24,128,128]{2,1,0:T(8,128)(2,1)S(1)}, bf16[24,128,128]{2,1,0:T(8,128)(2,1)S(1)}, u32[]{:S(2)}, u32[]{:S(2)}) collective-permute-start(bf16[24,128,128]{2,1,0:T(8,128)(2,1)S(1)} %get-tuple-element.17.rest_0_), channel_id=1, source_target_pairs={{0,2},{1,3},{2,0},{3,1},{4,6},{5,7},{6,4},{7,5},{8,10},{9,11},{10,... | collective-permute-start | bytes 2359304 | tf_op jit(solution)/shard_map/ppermute | solution.py:156
  35.5 16.9 %copy-start.6 = (bf16[128,1536]{1,0:T(8,128)(2,1)S(1)}, bf16[128,1536]{1,0:T(8,128)(2,1)}, u32[]{:S(2)}) copy-start(bf16[128,1536]{1,0:T(8,128)(2,1)} %dy.1) | copy-start | bytes 1179652
  44.9 106.4 %collective-permute-start.6 = (bf16[12,128,128]{2,1,0:T(8,128)(2,1)S(1)}, bf16[12,128,128]{2,1,0:T(8,128)(2,1)S(1)}, u32[]{:S(2)}, u32[]{:S(2)}) collective-permute-start(bf16[12,128,128]{2,1,0:T(8,128)(2,1)S(1)} %get-tuple-element.24), channel_id=1, source_target_pairs={{0,1},{1,0},{2,3},{3,2},{4,5},{5,4},{6,7},{7,6},{8,9},{9,8},{10,11... | collective-permute-start | bytes 1179656 | tf_op jit(solution)/shard_map/ppermute | solution.py:156
  46.4 104.9 %collective-permute-start.7 = (bf16[12,128,128]{2,1,0:T(8,128)(2,1)S(1)}, bf16[12,128,128]{2,1,0:T(8,128)(2,1)S(1)}, u32[]{:S(2)}, u32[]{:S(2)}) collective-permute-start(bf16[12,128,128]{2,1,0:T(8,128)(2,1)S(1)} %get-tuple-element.25), channel_id=1, source_target_pairs={{0,2},{1,3},{2,0},{3,1},{4,6},{5,7},{6,4},{7,5},{8,10},{9,11},{10,... | collective-permute-start | bytes 1179656 | tf_op jit(solution)/shard_map/ppermute | solution.py:156
  58.1 1.4 copy-start.2

commit v3 on v1

--- a/solution.py
+++ b/solution.py
@@ -174,6 +174,179 @@
         last = jnp.where(mine == 0, other, value)
         value = jnp.concatenate([first, last], axis=0)
     return value.reshape((1,) + part.shape)
+
+
+LAGS = (0, 2, 4, 5, 7, 9, 11)
+
+
+def stream_count(rows):
+    return next((n for n in (8, 6, 4, 3, 2, 1) if rows % (64 * n) == 0), 0)
+
+
+def sum_streams_body(count, streams, scale, *refs):
+    parts, outs = refs[:count], refs[count : 2 * count]
+    acc, stage, land_core, land_end, land_mid, send_sem, recv_sem = refs[2 * count :]
+    me = lax.axis_index("dp")
+    core = lax.rem(me, 2)
+    z = lax.div(me, 2)
+    inner = jnp.logical_or(z == 1, z == 2)
+    end = jnp.logical_or(z == 0, z == 3)
+    core_peer = me + 1 - 2 * core
+    edge_peer = me + 2 - 4 * lax.rem(z, 2)
+    mid_peer = me + 6 - 4 * z
+    part_mid = lax.div(z, 2)
+    half = parts[0].shape[0] // streams // 2
+    quarter = half // 2
+    total = count * streams
+    mesh_id = pl.DeviceIdType.MESH
+
+    barrier = pltpu.get_barrier_semaphore()
+    for peer in (core_peer, edge_peer):
+        pl.semaphore_signal(barrier, inc=1, device_id={"dp": peer}, device_id_type=mesh_id)
+
+    @pl.when(inner)
+    def _():
+        pl.semaphore_signal(barrier, inc=1, device_id={"dp": mid_peer}, device_id_type=mesh_id)
+        pl.semaphore_wait(barrier, 3)
+
+    @pl.when(end)
+    def _():
+        pl.semaphore_wait(barrier, 2)
+
+    def span(at, length):
+        return pl.ds(pl.multiple_of(at, 16), length)
+
+    def copy(j, kind):
+        which, base = j // streams, (j % streams) * 2 * half
+        own = span(base + core * half, half)
+        if kind == 0:
+            source = parts[which].at[span(base + (1 - core) * half, half)]
+            target, peer = land_core.at[j], core_peer
+        elif kind == 1:
+            source, target, peer = stage.at[j], land_end.at[j], edge_peer
+        elif kind == 2:
+            source = stage.at[j, span((1 - part_mid) * quarter, quarter)]
+            target, peer = land_mid.at[j], mid_peer
+        elif kind == 3:
+            source = outs[which].at[span(base + core * half + part_mid * quarter, quarter)]
+            target, peer = source, mid_peer
+        else:
+            source = target = outs[which].at[own]
+            peer = edge_peer if kind == 4 else core_peer
+        return pltpu.make_async_remote_copy(
+            src_ref=source,
+            dst_ref=target,
+            send_sem=send_sem.at[j, kind],
+            recv_sem=recv_sem.at[j, kind],
+            device_id={"dp": peer},
+            device_id_type=mesh_id,
+        )
+
+    def advance(j, step):
+        which, base = j // streams, (j % streams) * 2 * half
+        if step == 0:
+            copy(j, 0).start()
+        elif step == 1:
+            copy(j, 0).wait_recv()
+            own = parts[which][span(base + core * half, half)].astype(F32)
+            value = own + land_core[j].astype(F32)
+
+            @pl.when(end)
+            def _():
+                stage[j] = value.astype(BF16)
+                copy(j, 1).start()
+
+            @pl.when(inner)
+            def _():
+                acc[j] = value
+
+        elif step == 2:
+
+            @pl.when(inner)
+            def _():
+                copy(j, 1).wait_recv()
+                value = acc[j] + land_end[j].astype(F32)
+                acc[j] = value
+                stage[j] = value.astype(BF16)
+                copy(j, 2).start()
+
+        elif step == 3:
+
+            @pl.when(inner)
+            def _():
+                copy(j, 2).wait_recv()
+                held = acc[j, span(part_mid * quarter, quarter)]
+                value = held + land_mid[j].astype(F32)
+                place = span(base + core * half + part_mid * quarter, quarter)
+                outs[which][place] = (value * scale).astype(BF16)
+                copy(j, 3).start()
+
+        elif step == 4:
+
+            @pl.when(inner)
+            def _():
+                copy(j, 3).wait_recv()
+                copy(j, 4).start()
+                copy(j, 5).start()
+
+        elif step == 5:
+
+            @pl.when(end)
+            def _():
+                copy(j, 4).wait_recv()
+                copy(j, 5).start()
+
+        else:
+            copy(j, 5).wait_recv()
+
+    for tick in range(LAGS[-1] + total):
+        for j in range(total):
+            if tick - j in LAGS:
+                advance(j, LAGS.index(tick - j))
+    for j in range(total):
+        copy(j, 0).wait_send()
+        copy(j, 5).wait_send()
+
+    @pl.when(end)
+    def _():
+        for j in range(total):
+            copy(j, 1).wait_send()
+
+    @pl.when(inner)
+    def _():
+        for j in range(total):
+            for kind in (2, 3, 4):
+                copy(j, kind).wait_send()
+
+
+def token_sums(parts, scale):
+    flat = [p.reshape(-1, p.shape[-1]) for p in parts]
+    height, width = flat[0].shape
+    streams = stream_count(height)
+    if lax.axis_size("dp") != 8 or not streams or any(f.shape != flat[0].shape for f in flat):
+        return [token_sum(p, scale) for p in parts]
+    count, half = len(parts), height // streams // 2
+    total = count * streams
+    sums = pl.pallas_call(
+        functools.partial(sum_streams_body, count, streams, scale),
+        out_shape=[jax.ShapeDtypeStruct(f.shape, BF16) for f in flat],
+        in_specs=[VM] * count,
+        out_specs=[VM] * count,
+        scratch_shapes=[
+            pltpu.VMEM((total, half, width), F32),
+            pltpu.VMEM((total, half, width), BF16),
+            pltpu.VMEM((total, half, width), BF16),
+            pltpu.VMEM((total, half, width), BF16),
+            pltpu.VMEM((total, half // 2, width), BF16),
+            pltpu.SemaphoreType.DMA((total, 6)),
+            pltpu.SemaphoreType.DMA((total, 6)),
+        ],
+        compiler_params=pltpu.CompilerParams(
+            collective_id=0, has_side_effects=True, vmem_limit_bytes=48 * 2**20
+        ),
+        cost_estimate=pl.CostEstimate(flops=2**20, bytes_accessed=200 * 2**20, transcendentals=0),
+    )(*flat)
+    return [s.reshape((1,) + p.shape) for s, p in zip(sums, parts)]
 
 
 def local(inputs, up_weight, up_pick, down_weight, down_pick, cotangent):
@@ -217,8 +390,7 @@
         2 * macs, 12 * 2**20, [SM] + [VM] * (levels + 2),
     )(down_pick, *acts, down_weight, cotangent)
     backs = [back[0]] + [swap(back[b + 1], "mp", b) for b in range(bit_count)]
-    up_out = token_sum(up_part, scale)
-    down_out = token_sum(down_part, scale)
+    up_out, down_out = token_sums([up_part, down_part], scale)
     [grad_inputs] = call(
         functools.partial(sum_body, levels),
         [((tokens, width), BF16)], 2**20, 2 * 2**20, [VM] * levels,

time: 192 us -> 159 us (0.83); the launches traced: 188 us -> 158 us
  Pallas kernels: 26 us -> 119 us
  waiting for transfers between devices: 92.6 us -> 19.6 us
  other arithmetic: 24.5 us -> 0 us
  starting transfers between devices: 34 us -> 10.6 us
    pallas_call x0 -> x1, Pallas kernels: none -> 95.2 us  [token_sums(): pl.pallas_call(functools.partial(sum_streams_body, count, streams, scale)...]
    ppermute x20 -> x8, waiting for transfers between devices: 92.6 us -> 19.6 us  [swap(): return lax.ppermute(block, axis, [(i, i ^ 1 << bit) for i in range(count)])]
    ppermute x20 -> x8, starting transfers between devices: 34 us -> 10.6 us  [swap(): return lax.ppermute(block, axis, [(i, i ^ 1 << bit) for i in range(count)])]
    concatenate x6 -> x0, other arithmetic: 18.9 us -> none  [token_sum(): value = jnp.concatenate([first, last], axis=0)]
    dynamic_slice x2 -> x0, local copies, waits for them, and re-layouts: 3.02 us -> none  [token_sum(): sent = lax.dynamic_slice_in_dim(value, (1 - mine) * rows, rows).astype(BF16)]
    add x4 -> x0, other arithmetic: 2.99 us -> none  [token_sum(): value = kept + swap(sent, 'dp', bit).astype(F32)]
    unnamed x34 -> x20, local copies, waits for them, and re-layouts: 6.14 us -> 8.81 us
  transfers between devices with their start and end apart: 20 -> 8, of which waited for: 11 -> 4; matrix products, arithmetic and copies ran while one was open for 10% -> 0% of each run, Pallas kernels for 11% -> 74%
where the time goes in v3:
time: 159 us; the launch traced here: 158 us
  Pallas kernels  119 us (75%)
  waiting for transfers between devices  19.6 us (12%)
  starting transfers between devices  10.6 us (7%)
  local copies, waits for them, and re-layouts  8.81 us (6%)
    pallas_call x1, Pallas kernels, token_sums(): pl.pallas_call(functools.partial(sum_streams_body, count, streams, scale)...  95.2 us
    ppermute x8, waiting for transfers between devices, swap(): return lax.ppermute(block, axis, [(i, i ^ 1 << bit) for i in range(count)])  19.6 us
    ppermute x8, starting transfers between devices, swap(): return lax.ppermute(block, axis, [(i, i ^ 1 << bit) for i in range(count)])  10.6 us
    pallas_call x1, Pallas kernels, local(): call(functools.partial(mid_body, levels), [((levels, hid_blocks, size, si...  9.43 us
    unnamed x20, local copies, waits for them, and re-layouts  8.81 us
    pallas_call x1, Pallas kernels, local(): call(functools.partial(down_body, levels), [((tokens, width), BF16), ((le...  5.8 us
    pallas_call x1, Pallas kernels, local(): call(functools.partial(back_body, levels), [(hid, F32)] + [(hid, BF16)] *...  4.68 us
  transfers between devices with their start and end apart: 8, of which 4 were waited for; matrix products, arithmetic and copies ran while one was open for 0% of the time, Pallas kernels for 74%

profile of v3, /device:TPU:0, one launch (start us, length us, event | category | flops | bytes accessed | tf_op | source)
XLA Modules:
  0.0 158.5 jit_solution(7167295828739808963)
XLA Ops:
  0.6 3.0 %collective-permute-start = (bf16[128,1536]{1,0:T(8,128)(2,1)}, bf16[128,1536]{1,0:T(8,128)(2,1)S(1)}, u32[]{:S(2)}, u32[]{:S(2)}) collective-permute-start(bf16[128,1536]{1,0:T(8,128)(2,1)} %rest_0_.3), channel_id=1, source_target_pairs={{0,1},{1,0},{2,3},{3,2},{4,5},{5,4},{6,7},{7,6},{8,9},{9,8},{10,11... | collective-permute-start | bytes 1179656 | tf_op jit(solution)/shard_map/ppermute | solution.py:156
  3.6 1.5 collective-permute-start.1
  5.2 0.8 copy.11.pick
  6.0 1.7 %copy-done.1 = bf16[1,3,12,2,128,128]{5,4,3,2,1,0:T(8,128)(2,1)S(1)} copy-done((bf16[1,3,12,2,128,128]{5,4,3,2,1,0:T(8,128)(2,1)S(1)}, bf16[1,3,12,2,128,128]{5,4,3,2,1,0:T(8,128)(2,1)}, u32[]{:S(2)}) %copy-start.1) | copy-done | bytes 2359320
  7.6 1.0 copy-done.5
  8.6 4.7 %shard_map.95 = (f32[24,128,128]{2,1,0:T(8,128)S(1)}, bf16[24,128,128]{2,1,0:T(8,128)(2,1)S(1)}, bf16[24,128,128]{2,1,0:T(8,128)(2,1)S(1)}) custom-call(s32[1,3,12,2]{3,2,1,0:T(8,128)S(1)} %copy.11.pick, bf16[128,1536]{1,0:T(8,128)(2,1)S(1)} %copy-done.5, bf16[1,3,12,2,128,128]{5,4,3,2,1,0:T(8,128)(2,1)S(1)} %copy-done.1), custom_call_target="tpu_custom_call" | custom-call | flops 301989888 | bytes 8388608 | tf_op jit(solution)/shard_map/pallas_call | solution.py:364
  13.3 1.1 copy-done.4
  14.4 0.5 collective-permute-start.4
  15.1 2.7 %shard_map.93 = (f32[24,128,128]{2,1,0:T(8,128)S(1)}, bf16[24,128,128]{2,1,0:T(8,128)(2,1)S(1)}) custom-call(s32[1,3,24]{2,1,0:T(4,128)S(1)} %copy.10.pick, bf16[128,1536]{1,0:T(8,128)(2,1)S(1)} %copy-done.3, bf16[128,1536]{1,0:T(8,128)(2,1)S(1)} %collective-permute-done.rest_1_, bf16[128,1536]{1,0:T(8,128)(2,1)S(1)} %collective-permute-done.1.rest_2_, ...), custom_call_target="tpu_custom_call" | custom-call | flops 301989888 | bytes 8388608 | tf_op jit(solution)/shard_map/pallas_call | solution.py:371
  17.8 2.0 %collective-permute-start.2 = (bf16[24,128,128]{2,1,0:T(8,128)(2,1)S(1)}, bf16[24,128,128]{2,1,0:T(8,128)(2,1)S(1)}, u32[]{:S(2)}, u32[]{:S(2)}) collective-permute-start(bf16[24,128,128]{2,1,0:T(8,128)(2,1)S(1)} %get-tuple-element.17.rest_0_), channel_id=1, source_target_pairs={{0,1},{1,0},{2,3},{3,2},{4,5},{5,4},{6,7},{7,6},{8,9},{9,8},{10,11... | collective-permute-start | bytes 2359304 | tf_op jit(solution)/shard_map/ppermute | solution.py:156
  19.8 1.5 collective-permute-start.3
  21.3 13.7 %collective-permute-done.4.rest_6_ = bf16[24,128,128]{2,1,0:T(8,128)(2,1)S(1)} collective-permute-done((bf16[24,128,128]{2,1,0:T(8,128)(2,1)S(1)}, bf16[24,128,128]{2,1,0:T(8,128)(2,1)S(1)}, u32[]{:S(2)}, u32[]{:S(2)}) %collective-permute-start.4) | collective-permute-done | bytes 786464 | tf_op jit(solution)/shard_map/ppermute | solution.py:156
  34.9 0.5 collective-permute-done.5.rest_7_
  35.5 9.4 %shard_map.96 = (bf16[3,24,128,128]{3,2,1,0:T(8,128)(2,1)}, f32[12,128,128]{2,1,0:T(8,128)S(1)}, bf16[12,128,128]{2,1,0:T(8,128)(2,1)S(1)}, bf16[12,128,128]{2,1,0:T(8,128)(2,1)S(1)}) custom-call(s32[1,3,24]{2,1,0:T(4,128)S(1)} %copy.10.pick, bf16[128,1536]{1,0:T(8,128)(2,1)S(1)} %copy-done.3, bf16[128,1536]{1,0:T(8,128)(2,1)S(1)} %collective-permute-done.rest_1_, ...), custom_call_target="tpu_custom_call" | custom-call | flops 603979776 | bytes 16777216 | tf_op jit(solution)/shard_map/pallas_call | solution.py:377
  44.9 1.5 collective-permute-start.6
  46.4 0.5 collective-permute-start.7
  46.9 4.9 %collective-permute-done.2.rest_1_ = bf16[24,128,128]{2,1,0:T(8,128)(2,1)S(1)} collective-permute-done((bf16[24,128,128]{2,1,0:T(8,128)(2,1)S(1)}, bf16[24,128,128]{2,1,0:T(8,128)(2,1)S(1)}, u32[]{:S(2)}, u32[]{:S(2)}) %collective-permute-start.2) | collective-permute-done | bytes 786464 | tf_op jit(solution)/shard_map/ppermute | solution.py:156
  51.8 0.5 collective-permute-done.3.rest_2_
  52.3 5.8 %shard_map.94 = (bf16[128,1536]{1,0:T(8,128)(2,1)}, bf16[3,12,2,128,128]{4,3,2,1,0:T(8,128)(2,1)S(1)}) custom-call(s32[1,3,12,2]{3,2,1,0:T(8,128)S(1)} %copy.11.pick, bf16[24,128,128]{2,1,0:T(8,128)(2,1)S(1)} %get-tuple-element.17.rest_0_, bf16[24,128,128]{2,1,0:T(8,128)(2,1)S(1)} %collective-permute-done.2.rest_1_, ...), custom_call_target="tpu_custom_call" | custom-call | flops 603979776 | bytes 12582912 | tf_op jit(solution)/shard_map/pallas_call | solution.py:387
  58.1 1.4 copy-done.2
  59.5 95.2 %shard_map.98 = (bf16[9216,128]{1,0:T(8,128)(2,1)S(1)}, bf16[9216,128]{1,0:T(8,128)(2,1)S(1)}) custom-call(bf16[9216,128]{1,0:T(8,128)(2,1)} %bitcast.7, bf16[9216,128]{1,0:T(8,128)(2,1)} %bitcast.6), custom_call_target="tpu_custom_call" | custom-call | flops 1048576 | bytes 209715200 | tf_op jit(solution)/shard_map/pallas_call | solution.py:330
  154.8 0.9 shard_map.97
  155.7 1.4 copy.16
  157.1 1.4 copy.17
  (18 shorter events, 0.1 us)
Async XLA Ops:
  0.6 14.5 %copy-start = (bf16[1,3,24,128,128]{4,3,2,1,0:T(8,128)(2,1)S(1)}, bf16[1,3,24,128,128]{4,3,2,1,0:T(8,128)(2,1)}, u32[]{:S(2)}) copy-start(bf16[1,3,24,128,128]{4,3,2,1,0:T(8,128)(2,1)} %rest_3_.5) | copy-start | bytes 7077892
  0.6 14.4 %collective-permute-start = (bf16[128,1536]{1,0:T(8,128)(2,1)}, bf16[128,1536]{1,0:T(8,128)(2,1)S(1)}, u32[]{:S(2)}, u32[]{:S(2)}) collective-permute-start(bf16[128,1536]{1,0:T(8,128)(2,1)} %rest_0_.3), channel_id=1, source_target_pairs={{0,1},{1,0},{2,3},{3,2},{4,5},{5,4},{6,7},{7,6},{8,9},{9,8},{10,11... | collective-permute-start | bytes 1179656 | tf_op jit(solution)/shard_map/ppermute | solution.py:156
  3.6 11.4 %collective-permute-start.1 = (bf16[128,1536]{1,0:T(8,128)(2,1)}, bf16[128,1536]{1,0:T(8,128)(2,1)S(1)}, u32[]{:S(2)}, u32[]{:S(2)}) collective-permute-start(bf16[128,1536]{1,0:T(8,128)(2,1)} %rest_0_.3), channel_id=1, source_target_pairs={{0,2},{1,3},{2,0},{3,1},{4,6},{5,7},{6,4},{7,5},{8,10},{9,11},{10,... | collective-permute-start | bytes 1179656 | tf_op jit(solution)/shard_map/ppermute | solution.py:156
  6.0 1.7 %copy-start.1 = (bf16[1,3,12,2,128,128]{5,4,3,2,1,0:T(8,128)(2,1)S(1)}, bf16[1,3,12,2,128,128]{5,4,3,2,1,0:T(8,128)(2,1)}, u32[]{:S(2)}) copy-start(bf16[1,3,12,2,128,128]{5,4,3,2,1,0:T(8,128)(2,1)} %weight.1) | copy-start | bytes 7077892
  7.6 1.0 copy-start.5
  8.6 6.5 %copy-start.7 = (s32[1,3,24]{2,0,1:T(1,128)S(1)}, s32[1,3,24]{2,0,1:T(1,128)}, u32[]{:S(2)}) copy-start(s32[1,3,24]{2,0,1:T(1,128)} %param.8) | copy-start | bytes 868
  8.6 6.5 %copy-start.3 = (bf16[128,1536]{1,0:T(8,128)(2,1)S(1)}, bf16[128,1536]{1,0:T(8,128)(2,1)}, u32[]{:S(2)}) copy-start(bf16[128,1536]{1,0:T(8,128)(2,1)} %rest_0_.3) | copy-start | bytes 1179652
  13.3 1.1 copy-start.4
  14.4 20.5 %collective-permute-start.4 = (bf16[24,128,128]{2,1,0:T(8,128)(2,1)S(1)}, bf16[24,128,128]{2,1,0:T(8,128)(2,1)S(1)}, u32[]{:S(2)}, u32[]{:S(2)}) collective-permute-start(bf16[24,128,128]{2,1,0:T(8,128)(2,1)S(1)} %get-tuple-element.21), channel_id=1, source_target_pairs={{0,1},{1,0},{2,3},{3,2},{4,5},{5,4},{6,7},{7,6},{8,9},{9,8},{10,11... | collective-permute-start | bytes 2359304 | tf_op jit(solution)/shard_map/ppermute | solution.py:156
  15.0 20.5 %collective-permute-start.5 = (bf16[24,128,128]{2,1,0:T(8,128)(2,1)S(1)}, bf16[24,128,128]{2,1,0:T(8,128)(2,1)S(1)}, u32[]{:S(2)}, u32[]{:S(2)}) collective-permute-start(bf16[24,128,128]{2,1,0:T(8,128)(2,1)S(1)} %get-tuple-element.22), channel_id=1, source_target_pairs={{0,2},{1,3},{2,0},{3,1},{4,6},{5,7},{6,4},{7,5},{8,10},{9,11},{10,... | collective-permute-start | bytes 2359304 | tf_op jit(solution)/shard_map/ppermute | solution.py:156
  17.8 34.0 %collective-permute-start.2 = (bf16[24,128,128]{2,1,0:T(8,128)(2,1)S(1)}, bf16[24,128,128]{2,1,0:T(8,128)(2,1)S(1)}, u32[]{:S(2)}, u32[]{:S(2)}) collective-permute-start(bf16[24,128,128]{2,1,0:T(8,128)(2,1)S(1)} %get-tuple-element.17.rest_0_), channel_id=1, source_target_pairs={{0,1},{1,0},{2,3},{3,2},{4,5},{5,4},{6,7},{7,6},{8,9},{9,8},{10,11... | collective-permute-start | bytes 2359304 | tf_op jit(solution)/shard_map/ppermute | solution.py:156
  19.8 32.6 %collective-permute-start.3 = (bf16[24,128,128]{2,1,0:T(8,128)(2,1)S(1)}, bf16[24,128,128]{2,1,0:T(8,128)(2,1)S(1)}, u32[]{:S(2)}, u32[]{:S(2)}) collective-permute-start(bf16[24,128,128]{2,1,0:T(8,128)(2,1)S(1)} %get-tuple-element.17.rest_0_), channel_id=1, source_target_pairs={{0,2},{1,3},{2,0},{3,1},{4,6},{5,7},{6,4},{7,5},{8,10},{9,11},{10,... | collective-permute-start | bytes 2359304 | tf_op jit(solution)/shard_map/ppermute | solution.py:156
  35.5 16.9 %copy-start.6 = (bf16[128,1536]{1,0:T(8,128)(2,1)S(1)}, bf16[128,1536]{1,0:T(8,128)(2,1)}, u32[]{:S(2)}) copy-start(bf16[128,1536]{1,0:T(8,128)(2,1)} %dy.1) | copy-start | bytes 1179652
  44.9 109.9 %collective-permute-start.6 = (bf16[12,128,128]{2,1,0:T(8,128)(2,1)S(1)}, bf16[12,128,128]{2,1,0:T(8,128)(2,1)S(1)}, u32[]{:S(2)}, u32[]{:S(2)}) collective-permute-start(bf16[12,128,128]{2,1,0:T(8,128)(2,1)S(1)} %get-tuple-element.24), channel_id=1, source_target_pairs={{0,1},{1,0},{2,3},{3,2},{4,5},{5,4},{6,7},{7,6},{8,9},{9,8},{10,11... | collective-permute-start | bytes 1179656 | tf_op jit(solution)/shard_map/ppermute | solution.py:156
  46.4 108.4 %collective-permute-start.7 = (bf16[12,128,128]{2,1,0:T(8,128)(2,1)S(1)}, bf16[12,128,128]{2,1,0:T(8,128)(2,1)S(1)}, u32[]{:S(2)}, u32[]{:S(2)}) collective-permute-start(bf16[12,128,128]{2,1,0:T(8,128)(2,1)S(1)} %get-tuple-element.25), channel_id=1, source_target_pairs={{0,2},{1,3},{2,0},{3,1},{4,6},{5,7},{6,4},{7,5},{8,10},{9,11},{10,... | collective-permute-start | bytes 1179656 | tf_op jit(solution)/shard_map/ppermute | solution.py:156
  58.1 1.4 copy-start.2

commit v4 on v2

--- a/solution.py
+++ b/solution.py
@@ -177,7 +177,7 @@
 
 
 def stream_count(rows, devices):
-    return next((n for n in (4, 2, 1) if rows % (16 * devices * n) == 0), 0)
+    return next((n for n in (6, 4, 3, 2, 1) if rows % (16 * devices * n) == 0), 0)
 
 
 def sum_streams_body(count, streams, bits, scale, *refs):
@@ -262,7 +262,7 @@
             copy(j, step).wait_send()
 
 
-def token_sums(parts, scale):
+def token_sums(parts, scale, call_id):
     devices = lax.axis_size("dp")
     bits = devices.bit_length() - 1
     flat = [p.reshape(-1, p.shape[-1]) for p in parts]
@@ -286,7 +286,7 @@
             pltpu.SemaphoreType.DMA((total, 2 * bits)),
         ],
         compiler_params=pltpu.CompilerParams(
-            collective_id=0, has_side_effects=True, vmem_limit_bytes=48 * 2**20
+            collective_id=call_id, has_side_effects=True, vmem_limit_bytes=48 * 2**20
         ),
         cost_estimate=pl.CostEstimate(flops=2**20, bytes_accessed=200 * 2**20, transcendentals=0),
     )(*flat)
@@ -328,13 +328,15 @@
         ],
     )(up_pick, *sources, up_weight, hidden, *grads)
     up_part, back = mid[0], mid[1:]
+    backs = [back[0]] + [swap(back[b + 1], "mp", b) for b in range(bit_count)]
+    [up_out] = token_sums([up_part], scale, 0)
+    up_out, down_pick = lax.optimization_barrier((up_out, down_pick))
     result, down_part = call(
         functools.partial(down_body, levels),
         [((tokens, width), BF16), ((levels, in_blocks, slots, size, size), BF16)],
         2 * macs, 12 * 2**20, [SM] + [VM] * (levels + 2),
     )(down_pick, *acts, down_weight, cotangent)
-    backs = [back[0]] + [swap(back[b + 1], "mp", b) for b in range(bit_count)]
-    up_out, down_out = token_sums([up_part, down_part], scale)
+    [down_out] = token_sums([down_part], scale, 1)
     [grad_inputs] = call(
         functools.partial(sum_body, levels),
         [((tokens, width), BF16)], 2**20, 2 * 2**20, [VM] * levels,

time: 155 us -> 163 us (1.052)
  Pallas kernels: 115 us -> 128 us
  waiting for transfers between devices: 19.6 us -> 13.4 us
  local copies, waits for them, and re-layouts: 8.81 us -> 10.5 us
    pallas_call x1 -> x2, Pallas kernels: 91.8 us -> 103 us  [token_sums(): pl.pallas_call(functools.partial(sum_streams_body, count, streams, bits,...]
    ppermute x8, waiting for transfers between devices: 19.6 us -> 13.4 us  [swap(): return lax.ppermute(block, axis, [(i, i ^ 1 << bit) for i in range(count)])]
    unnamed x20 -> x28, local copies, waits for them, and re-layouts: 8.81 us -> 9.82 us
  transfers between devices with their start and end apart: 8 -> 8, of which waited for: 4 -> 2; matrix products, arithmetic and copies ran while one was open for 1% -> 1% of each run, Pallas kernels for 74% -> 78%
where the time goes in v4:
time: 163 us
  Pallas kernels  128 us (79%)
  waiting for transfers between devices  13.4 us (8%)
  local copies, waits for them, and re-layouts  10.5 us (6%)
  starting transfers between devices  10.5 us (6%)
    pallas_call x2, Pallas kernels, token_sums(): pl.pallas_call(functools.partial(sum_streams_body, count, streams, bits,...  103 us
    ppermute x8, waiting for transfers between devices, swap(): return lax.ppermute(block, axis, [(i, i ^ 1 << bit) for i in range(count)])  13.4 us
    ppermute x8, starting transfers between devices, swap(): return lax.ppermute(block, axis, [(i, i ^ 1 << bit) for i in range(count)])  10.5 us
    unnamed x28, local copies, waits for them, and re-layouts  9.82 us
    pallas_call x1, Pallas kernels, local(): call(functools.partial(mid_body, levels), [((levels, hid_blocks, size, si...  9.68 us
    pallas_call x1, Pallas kernels, local(): call(functools.partial(down_body, levels), [((tokens, width), BF16), ((le...  6.5 us
    pallas_call x1, Pallas kernels, local(): call(functools.partial(back_body, levels), [(hid, F32)] + [(hid, BF16)] *...  4.69 us
    pallas_call x1, Pallas kernels, local(): call(functools.partial(up_body, levels), [(hid, F32), (hid, BF16)], macs,...  3.56 us
  transfers between devices with their start and end apart: 8, of which 2 were waited for; matrix products, arithmetic and copies ran while one was open for 1% of the time, Pallas kernels for 78%

profile of v4, /device:TPU:0, one launch (start us, length us, event | category | flops | bytes accessed | tf_op | source)
XLA Modules:
  0.0 163.1 jit_solution(14860528729509865349)
XLA Ops:
  0.6 3.0 %collective-permute-start = (bf16[128,1536]{1,0:T(8,128)(2,1)}, bf16[128,1536]{1,0:T(8,128)(2,1)S(1)}, u32[]{:S(2)}, u32[]{:S(2)}) collective-permute-start(bf16[128,1536]{1,0:T(8,128)(2,1)} %rest_0_.3), channel_id=1, source_target_pairs={{0,1},{1,0},{2,3},{3,2},{4,5},{5,4},{6,7},{7,6},{8,9},{9,8},{10,11... | collective-permute-start | bytes 1179656 | tf_op jit(solution)/shard_map/ppermute | solution.py:156
  3.6 1.5 collective-permute-start.1
  5.2 0.8 copy.11.pick
  6.0 1.7 %copy-done.1 = bf16[1,3,12,2,128,128]{5,4,3,2,1,0:T(8,128)(2,1)S(1)} copy-done((bf16[1,3,12,2,128,128]{5,4,3,2,1,0:T(8,128)(2,1)S(1)}, bf16[1,3,12,2,128,128]{5,4,3,2,1,0:T(8,128)(2,1)}, u32[]{:S(2)}) %copy-start.1) | copy-done | bytes 2359320
  7.6 1.0 copy-done.5
  8.6 4.7 %shard_map.94 = (f32[24,128,128]{2,1,0:T(8,128)S(1)}, bf16[24,128,128]{2,1,0:T(8,128)(2,1)S(1)}, bf16[24,128,128]{2,1,0:T(8,128)(2,1)S(1)}) custom-call(s32[1,3,12,2]{3,2,1,0:T(8,128)S(1)} %copy.11.pick, bf16[128,1536]{1,0:T(8,128)(2,1)S(1)} %copy-done.5, bf16[1,3,12,2,128,128]{5,4,3,2,1,0:T(8,128)(2,1)S(1)} %copy-done.1), custom_call_target="tpu_custom_call" | custom-call | flops 301989888 | bytes 8388608 | tf_op jit(solution)/shard_map/pallas_call | solution.py:308
  13.3 1.1 copy-done.4
  14.5 0.5 collective-permute-start.2
  15.1 3.6 %shard_map.93 = (f32[24,128,128]{2,1,0:T(8,128)S(1)}, bf16[24,128,128]{2,1,0:T(8,128)(2,1)}) custom-call(s32[1,3,24]{2,1,0:T(4,128)S(1)} %copy.12.pick, bf16[128,1536]{1,0:T(8,128)(2,1)S(1)} %copy-done.3, bf16[128,1536]{1,0:T(8,128)(2,1)S(1)} %collective-permute-done.rest_1_, bf16[128,1536]{1,0:T(8,128)(2,1)S(1)} %collective-permute-done.1.rest_2_, ...), custom_call_target="tpu_custom_call" | custom-call | flops 301989888 | bytes 8388608 | tf_op jit(solution)/shard_map/pallas_call | solution.py:315
  18.7 1.9 %collective-permute-start.4 = (bf16[24,128,128]{2,1,0:T(8,128)(2,1)}, bf16[24,128,128]{2,1,0:T(8,128)(2,1)}, u32[]{:S(2)}, u32[]{:S(2)}) collective-permute-start(bf16[24,128,128]{2,1,0:T(8,128)(2,1)} %get-tuple-element.23.rest_0_), channel_id=1, source_target_pairs={{0,1},{1,0},{2,3},{3,2},{4,5},{5,4},{6,7},{7,6},{8,9},{9,8},{10,11... | collective-permute-start | bytes 2359304 | tf_op jit(solution)/shard_map/ppermute | solution.py:156
  20.6 1.5 collective-permute-start.5
  22.1 12.8 %collective-permute-done.2.rest_6_ = bf16[24,128,128]{2,1,0:T(8,128)(2,1)S(1)} collective-permute-done((bf16[24,128,128]{2,1,0:T(8,128)(2,1)S(1)}, bf16[24,128,128]{2,1,0:T(8,128)(2,1)S(1)}, u32[]{:S(2)}, u32[]{:S(2)}) %collective-permute-start.2) | collective-permute-done | bytes 786464 | tf_op jit(solution)/shard_map/ppermute | solution.py:156
  34.9 0.5 collective-permute-done.3.rest_7_
  35.5 9.7 %shard_map.95 = (bf16[3,24,128,128]{3,2,1,0:T(8,128)(2,1)}, f32[12,128,128]{2,1,0:T(8,128)S(1)}, bf16[12,128,128]{2,1,0:T(8,128)(2,1)}, bf16[12,128,128]{2,1,0:T(8,128)(2,1)}) custom-call(s32[1,3,24]{2,1,0:T(4,128)S(1)} %copy.12.pick, bf16[128,1536]{1,0:T(8,128)(2,1)S(1)} %copy-done.3, bf16[128,1536]{1,0:T(8,128)(2,1)S(1)} %collective-permute-done.rest_1_, ...), custom_call_target="tpu_custom_call" | custom-call | flops 603979776 | bytes 16777216 | tf_op jit(solution)/shard_map/pallas_call | solution.py:321
  45.1 1.5 collective-permute-start.6
  47.1 1.7 %copy-done.2 = bf16[3,24,128,128]{3,2,1,0:T(8,128)(2,1)S(1)} copy-done((bf16[3,24,128,128]{3,2,1,0:T(8,128)(2,1)S(1)}, bf16[3,24,128,128]{3,2,1,0:T(8,128)(2,1)}, u32[]{:S(2)}) %copy-start.2) | copy-done | bytes 2359320
  48.8 51.3 %shard_map.96 = bf16[9216,128]{1,0:T(8,128)(2,1)S(1)} custom-call(bf16[9216,128]{1,0:T(8,128)(2,1)S(1)} %bitcast.6), custom_call_target="tpu_custom_call" | custom-call | flops 1048576 | bytes 209715200 | tf_op jit(solution)/shard_map/pallas_call | solution.py:276
  100.0 0.7 copy.13.pick
  100.8 0.7 copy-done.9
  101.5 6.5 %shard_map.97 = (bf16[128,1536]{1,0:T(8,128)(2,1)}, bf16[3,12,2,128,128]{4,3,2,1,0:T(8,128)(2,1)S(1)}) custom-call(s32[1,3,12,2]{3,2,1,0:T(8,128)S(1)} %copy-done.9, bf16[24,128,128]{2,1,0:T(8,128)(2,1)} %get-tuple-element.23.rest_0_, bf16[24,128,128]{2,1,0:T(8,128)(2,1)} %collective-permute-done.4.rest_1_, ...), custom_call_target="tpu_custom_call" | custom-call | flops 603979776 | bytes 12582912 | tf_op jit(solution)/shard_map/pallas_call | solution.py:334
  108.0 51.4 %shard_map.99 = bf16[9216,128]{1,0:T(8,128)(2,1)S(1)} custom-call(bf16[9216,128]{1,0:T(8,128)(2,1)S(1)} %bitcast.7), custom_call_target="tpu_custom_call" | custom-call | flops 1048576 | bytes 209715200 | tf_op jit(solution)/shard_map/pallas_call | solution.py:276
  159.4 0.9 shard_map.98
  160.3 1.4 copy.16
  161.7 1.4 copy.17
  (28 shorter events, 0.6 us)
Async XLA Ops:
  0.6 14.5 %copy-start = (bf16[1,3,24,128,128]{4,3,2,1,0:T(8,128)(2,1)S(1)}, bf16[1,3,24,128,128]{4,3,2,1,0:T(8,128)(2,1)}, u32[]{:S(2)}) copy-start(bf16[1,3,24,128,128]{4,3,2,1,0:T(8,128)(2,1)} %rest_3_.4) | copy-start | bytes 7077892
  0.6 14.4 %collective-permute-start = (bf16[128,1536]{1,0:T(8,128)(2,1)}, bf16[128,1536]{1,0:T(8,128)(2,1)S(1)}, u32[]{:S(2)}, u32[]{:S(2)}) collective-permute-start(bf16[128,1536]{1,0:T(8,128)(2,1)} %rest_0_.3), channel_id=1, source_target_pairs={{0,1},{1,0},{2,3},{3,2},{4,5},{5,4},{6,7},{7,6},{8,9},{9,8},{10,11... | collective-permute-start | bytes 1179656 | tf_op jit(solution)/shard_map/ppermute | solution.py:156
  3.6 11.4 %collective-permute-start.1 = (bf16[128,1536]{1,0:T(8,128)(2,1)}, bf16[128,1536]{1,0:T(8,128)(2,1)S(1)}, u32[]{:S(2)}, u32[]{:S(2)}) collective-permute-start(bf16[128,1536]{1,0:T(8,128)(2,1)} %rest_0_.3), channel_id=1, source_target_pairs={{0,2},{1,3},{2,0},{3,1},{4,6},{5,7},{6,4},{7,5},{8,10},{9,11},{10,... | collective-permute-start | bytes 1179656 | tf_op jit(solution)/shard_map/ppermute | solution.py:156
  6.0 1.7 %copy-start.1 = (bf16[1,3,12,2,128,128]{5,4,3,2,1,0:T(8,128)(2,1)S(1)}, bf16[1,3,12,2,128,128]{5,4,3,2,1,0:T(8,128)(2,1)}, u32[]{:S(2)}) copy-start(bf16[1,3,12,2,128,128]{5,4,3,2,1,0:T(8,128)(2,1)} %rest_3_.5) | copy-start | bytes 7077892
  7.6 1.0 copy-start.5
  8.6 6.5 %copy-start.11 = (s32[1,3,24]{2,0,1:T(1,128)S(1)}, s32[1,3,24]{2,0,1:T(1,128)}, u32[]{:S(2)}) copy-start(s32[1,3,24]{2,0,1:T(1,128)} %param.8) | copy-start | bytes 868
  8.6 6.5 %copy-start.3 = (bf16[128,1536]{1,0:T(8,128)(2,1)S(1)}, bf16[128,1536]{1,0:T(8,128)(2,1)}, u32[]{:S(2)}) copy-start(bf16[128,1536]{1,0:T(8,128)(2,1)} %rest_0_.3) | copy-start | bytes 1179652
  13.3 1.1 copy-start.4
  14.5 20.5 %collective-permute-start.2 = (bf16[24,128,128]{2,1,0:T(8,128)(2,1)S(1)}, bf16[24,128,128]{2,1,0:T(8,128)(2,1)S(1)}, u32[]{:S(2)}, u32[]{:S(2)}) collective-permute-start(bf16[24,128,128]{2,1,0:T(8,128)(2,1)S(1)} %get-tuple-element.19), channel_id=1, source_target_pairs={{0,1},{1,0},{2,3},{3,2},{4,5},{5,4},{6,7},{7,6},{8,9},{9,8},{10,11... | collective-permute-start | bytes 2359304 | tf_op jit(solution)/shard_map/ppermute | solution.py:156
  15.0 20.5 %collective-permute-start.3 = (bf16[24,128,128]{2,1,0:T(8,128)(2,1)S(1)}, bf16[24,128,128]{2,1,0:T(8,128)(2,1)S(1)}, u32[]{:S(2)}, u32[]{:S(2)}) collective-permute-start(bf16[24,128,128]{2,1,0:T(8,128)(2,1)S(1)} %get-tuple-element.20), channel_id=1, source_target_pairs={{0,2},{1,3},{2,0},{3,1},{4,6},{5,7},{6,4},{7,5},{8,10},{9,11},{10,... | collective-permute-start | bytes 2359304 | tf_op jit(solution)/shard_map/ppermute | solution.py:156
  18.7 82.1 %collective-permute-start.4 = (bf16[24,128,128]{2,1,0:T(8,128)(2,1)}, bf16[24,128,128]{2,1,0:T(8,128)(2,1)}, u32[]{:S(2)}, u32[]{:S(2)}) collective-permute-start(bf16[24,128,128]{2,1,0:T(8,128)(2,1)} %get-tuple-element.23.rest_0_), channel_id=1, source_target_pairs={{0,1},{1,0},{2,3},{3,2},{4,5},{5,4},{6,7},{7,6},{8,9},{9,8},{10,11... | collective-permute-start | bytes 2359304 | tf_op jit(solution)/shard_map/ppermute | solution.py:156
  20.6 80.2 %collective-permute-start.5 = (bf16[24,128,128]{2,1,0:T(8,128)(2,1)}, bf16[24,128,128]{2,1,0:T(8,128)(2,1)}, u32[]{:S(2)}, u32[]{:S(2)}) collective-permute-start(bf16[24,128,128]{2,1,0:T(8,128)(2,1)} %get-tuple-element.23.rest_0_), channel_id=1, source_target_pairs={{0,2},{1,3},{2,0},{3,1},{4,6},{5,7},{6,4},{7,5},{8,10},{9,11},{10,... | collective-permute-start | bytes 2359304 | tf_op jit(solution)/shard_map/ppermute | solution.py:156
  45.1 54.9 %copy-start.7 = (f32[12,128,128]{2,1,0:T(8,128)}, f32[12,128,128]{2,1,0:T(8,128)S(1)}, u32[]{:S(2)}) copy-start(f32[12,128,128]{2,1,0:T(8,128)S(1)} %get-tuple-element.25.rest_0_) | copy-start | bytes 2359300
  45.1 114.2 %collective-permute-start.6 = (bf16[12,128,128]{2,1,0:T(8,128)(2,1)}, bf16[12,128,128]{2,1,0:T(8,128)(2,1)S(1)}, u32[]{:S(2)}, u32[]{:S(2)}) collective-permute-start(bf16[12,128,128]{2,1,0:T(8,128)(2,1)} %get-tuple-element.26), channel_id=1, source_target_pairs={{0,1},{1,0},{2,3},{3,2},{4,5},{5,4},{6,7},{7,6},{8,9},{9,8},{10,11... | collective-permute-start | bytes 1179656 | tf_op jit(solution)/shard_map/ppermute | solution.py:156
  46.7 112.7 %collective-permute-start.7 = (bf16[12,128,128]{2,1,0:T(8,128)(2,1)}, bf16[12,128,128]{2,1,0:T(8,128)(2,1)S(1)}, u32[]{:S(2)}, u32[]{:S(2)}) collective-permute-start(bf16[12,128,128]{2,1,0:T(8,128)(2,1)} %get-tuple-element.27), channel_id=1, source_target_pairs={{0,2},{1,3},{2,0},{3,1},{4,6},{5,7},{6,4},{7,5},{8,10},{9,11},{10,... | collective-permute-start | bytes 1179656 | tf_op jit(solution)/shard_map/ppermute | solution.py:156
  47.1 1.7 %copy-start.2 = (bf16[3,24,128,128]{3,2,1,0:T(8,128)(2,1)S(1)}, bf16[3,24,128,128]{3,2,1,0:T(8,128)(2,1)}, u32[]{:S(2)}) copy-start(bf16[3,24,128,128]{3,2,1,0:T(8,128)(2,1)} %get-tuple-element.21) | copy-start | bytes 7077892
  48.8 51.3 %copy-start.10 = (s32[1,3,12,2]{2,3,1,0:T(2,128)S(1)}, s32[1,3,12,2]{2,3,1,0:T(2,128)}, u32[]{:S(2)}) copy-start(s32[1,3,12,2]{2,3,1,0:T(2,128)} %param.10) | copy-start | bytes 868
  48.8 52.0 %copy-start.6 = (bf16[128,1536]{1,0:T(8,128)(2,1)S(1)}, bf16[128,1536]{1,0:T(8,128)(2,1)}, u32[]{:S(2)}) copy-start(bf16[128,1536]{1,0:T(8,128)(2,1)} %rest_4_.1) | copy-start | bytes 1179652
  100.8 0.7 copy-start.9
  108.0 51.4 %copy-start.8 = (f32[12,128,128]{2,1,0:T(8,128)S(1)}, f32[12,128,128]{2,1,0:T(8,128)}, u32[]{:S(2)}) copy-start(f32[12,128,128]{2,1,0:T(8,128)} %copy-done.7) | copy-start | bytes 2359300

commit v5 on v2

--- a/solution.py
+++ b/solution.py
@@ -177,7 +177,7 @@
 
 
 def stream_count(rows, devices):
-    return next((n for n in (4, 2, 1) if rows % (16 * devices * n) == 0), 0)
+    return next((n for n in (6, 4, 3, 2, 1) if rows % (16 * devices * n) == 0), 0)
 
 
 def sum_streams_body(count, streams, bits, scale, *refs):
@@ -253,10 +253,10 @@
         if step < 2 * bits:
             copy(j, step).start()
 
-    for tick in range(2 * bits + total):
+    for tick in range(4 * bits + total):
         for j in range(total):
-            if 0 <= tick - j <= 2 * bits:
-                advance(j, tick - j)
+            if 0 <= tick - j <= 4 * bits and (tick - j) % 2 == 0:
+                advance(j, (tick - j) // 2)
     for j in range(total):
         for step in range(2 * bits):
             copy(j, step).wait_send()

time: 155 us -> 150 us (0.968)
  Pallas kernels: 115 us -> 110 us
    pallas_call x1, Pallas kernels: 91.8 us -> 86.7 us  [token_sums(): pl.pallas_call(functools.partial(sum_streams_body, count, streams, bits,...]
  transfers between devices with their start and end apart: 8 -> 8, of which waited for: 4 -> 4; matrix products, arithmetic and copies ran while one was open for 1% -> 1% of each run, Pallas kernels for 74% -> 73%
where the time goes in v5:
time: 150 us
  Pallas kernels  110 us (73%)
  waiting for transfers between devices  19.6 us (13%)
  starting transfers between devices  10.6 us (7%)
  local copies, waits for them, and re-layouts  8.81 us (6%)
    pallas_call x1, Pallas kernels, token_sums(): pl.pallas_call(functools.partial(sum_streams_body, count, streams, bits,...  86.7 us
    ppermute x8, waiting for transfers between devices, swap(): return lax.ppermute(block, axis, [(i, i ^ 1 << bit) for i in range(count)])  19.6 us
    ppermute x8, starting transfers between devices, swap(): return lax.ppermute(block, axis, [(i, i ^ 1 << bit) for i in range(count)])  10.6 us
    pallas_call x1, Pallas kernels, local(): call(functools.partial(mid_body, levels), [((levels, hid_blocks, size, si...  9.48 us
    unnamed x20, local copies, waits for them, and re-layouts  8.81 us
    pallas_call x1, Pallas kernels, local(): call(functools.partial(down_body, levels), [((tokens, width), BF16), ((le...  5.8 us
    pallas_call x1, Pallas kernels, local(): call(functools.partial(back_body, levels), [(hid, F32)] + [(hid, BF16)] *...  4.68 us
  transfers between devices with their start and end apart: 8, of which 4 were waited for; matrix products, arithmetic and copies ran while one was open for 1% of the time, Pallas kernels for 73%

profile of v5, /device:TPU:0, one launch (start us, length us, event | category | flops | bytes accessed | tf_op | source)
XLA Modules:
  0.0 150.0 jit_solution(4135291999740009988)
XLA Ops:
  0.6 3.0 %collective-permute-start = (bf16[128,1536]{1,0:T(8,128)(2,1)}, bf16[128,1536]{1,0:T(8,128)(2,1)S(1)}, u32[]{:S(2)}, u32[]{:S(2)}) collective-permute-start(bf16[128,1536]{1,0:T(8,128)(2,1)} %rest_0_.3), channel_id=1, source_target_pairs={{0,1},{1,0},{2,3},{3,2},{4,5},{5,4},{6,7},{7,6},{8,9},{9,8},{10,11... | collective-permute-start | bytes 1179656 | tf_op jit(solution)/shard_map/ppermute | solution.py:156
  3.6 1.5 %collective-permute-start.1 = (bf16[128,1536]{1,0:T(8,128)(2,1)}, bf16[128,1536]{1,0:T(8,128)(2,1)S(1)}, u32[]{:S(2)}, u32[]{:S(2)}) collective-permute-start(bf16[128,1536]{1,0:T(8,128)(2,1)} %rest_0_.3), channel_id=1, source_target_pairs={{0,2},{1,3},{2,0},{3,1},{4,6},{5,7},{6,4},{7,5},{8,10},{9,11},{10,... | collective-permute-start | bytes 1179656 | tf_op jit(solution)/shard_map/ppermute | solution.py:156
  5.2 0.8 copy.11.pick
  6.0 1.7 %copy-done.1 = bf16[1,3,12,2,128,128]{5,4,3,2,1,0:T(8,128)(2,1)S(1)} copy-done((bf16[1,3,12,2,128,128]{5,4,3,2,1,0:T(8,128)(2,1)S(1)}, bf16[1,3,12,2,128,128]{5,4,3,2,1,0:T(8,128)(2,1)}, u32[]{:S(2)}) %copy-start.1) | copy-done | bytes 2359320
  7.6 1.0 copy-done.5
  8.6 4.7 %shard_map.95 = (f32[24,128,128]{2,1,0:T(8,128)S(1)}, bf16[24,128,128]{2,1,0:T(8,128)(2,1)S(1)}, bf16[24,128,128]{2,1,0:T(8,128)(2,1)S(1)}) custom-call(s32[1,3,12,2]{3,2,1,0:T(8,128)S(1)} %copy.11.pick, bf16[128,1536]{1,0:T(8,128)(2,1)S(1)} %copy-done.5, bf16[1,3,12,2,128,128]{5,4,3,2,1,0:T(8,128)(2,1)S(1)} %copy-done.1), custom_call_target="tpu_custom_call" | custom-call | flops 301989888 | bytes 8388608 | tf_op jit(solution)/shard_map/pallas_call | solution.py:308
  13.3 1.1 copy-done.4
  14.4 0.5 collective-permute-start.4
  15.1 2.7 %shard_map.93 = (f32[24,128,128]{2,1,0:T(8,128)S(1)}, bf16[24,128,128]{2,1,0:T(8,128)(2,1)S(1)}) custom-call(s32[1,3,24]{2,1,0:T(4,128)S(1)} %copy.10.pick, bf16[128,1536]{1,0:T(8,128)(2,1)S(1)} %copy-done.3, bf16[128,1536]{1,0:T(8,128)(2,1)S(1)} %collective-permute-done.rest_1_, bf16[128,1536]{1,0:T(8,128)(2,1)S(1)} %collective-permute-done.1.rest_2_, ...), custom_call_target="tpu_custom_call" | custom-call | flops 301989888 | bytes 8388608 | tf_op jit(solution)/shard_map/pallas_call | solution.py:315
  17.8 2.0 %collective-permute-start.2 = (bf16[24,128,128]{2,1,0:T(8,128)(2,1)S(1)}, bf16[24,128,128]{2,1,0:T(8,128)(2,1)S(1)}, u32[]{:S(2)}, u32[]{:S(2)}) collective-permute-start(bf16[24,128,128]{2,1,0:T(8,128)(2,1)S(1)} %get-tuple-element.17.rest_0_), channel_id=1, source_target_pairs={{0,1},{1,0},{2,3},{3,2},{4,5},{5,4},{6,7},{7,6},{8,9},{9,8},{10,11... | collective-permute-start | bytes 2359304 | tf_op jit(solution)/shard_map/ppermute | solution.py:156
  19.8 1.5 %collective-permute-start.3 = (bf16[24,128,128]{2,1,0:T(8,128)(2,1)S(1)}, bf16[24,128,128]{2,1,0:T(8,128)(2,1)S(1)}, u32[]{:S(2)}, u32[]{:S(2)}) collective-permute-start(bf16[24,128,128]{2,1,0:T(8,128)(2,1)S(1)} %get-tuple-element.17.rest_0_), channel_id=1, source_target_pairs={{0,2},{1,3},{2,0},{3,1},{4,6},{5,7},{6,4},{7,5},{8,10},{9,11},{10,... | collective-permute-start | bytes 2359304 | tf_op jit(solution)/shard_map/ppermute | solution.py:156
  21.3 13.7 %collective-permute-done.4.rest_6_ = bf16[24,128,128]{2,1,0:T(8,128)(2,1)S(1)} collective-permute-done((bf16[24,128,128]{2,1,0:T(8,128)(2,1)S(1)}, bf16[24,128,128]{2,1,0:T(8,128)(2,1)S(1)}, u32[]{:S(2)}, u32[]{:S(2)}) %collective-permute-start.4) | collective-permute-done | bytes 786464 | tf_op jit(solution)/shard_map/ppermute | solution.py:156
  34.9 0.5 collective-permute-done.5.rest_7_
  35.5 9.5 %shard_map.96 = (bf16[3,24,128,128]{3,2,1,0:T(8,128)(2,1)}, f32[12,128,128]{2,1,0:T(8,128)S(1)}, bf16[12,128,128]{2,1,0:T(8,128)(2,1)S(1)}, bf16[12,128,128]{2,1,0:T(8,128)(2,1)S(1)}) custom-call(s32[1,3,24]{2,1,0:T(4,128)S(1)} %copy.10.pick, bf16[128,1536]{1,0:T(8,128)(2,1)S(1)} %copy-done.3, bf16[128,1536]{1,0:T(8,128)(2,1)S(1)} %collective-permute-done.rest_1_, ...), custom_call_target="tpu_custom_call" | custom-call | flops 603979776 | bytes 16777216 | tf_op jit(solution)/shard_map/pallas_call | solution.py:321
  44.9 1.4 collective-permute-start.6
  46.4 0.5 collective-permute-start.7
  46.9 4.9 %collective-permute-done.2.rest_1_ = bf16[24,128,128]{2,1,0:T(8,128)(2,1)S(1)} collective-permute-done((bf16[24,128,128]{2,1,0:T(8,128)(2,1)S(1)}, bf16[24,128,128]{2,1,0:T(8,128)(2,1)S(1)}, u32[]{:S(2)}, u32[]{:S(2)}) %collective-permute-start.2) | collective-permute-done | bytes 786464 | tf_op jit(solution)/shard_map/ppermute | solution.py:156
  51.8 0.5 collective-permute-done.3.rest_2_
  52.3 5.8 %shard_map.94 = (bf16[128,1536]{1,0:T(8,128)(2,1)}, bf16[3,12,2,128,128]{4,3,2,1,0:T(8,128)(2,1)S(1)}) custom-call(s32[1,3,12,2]{3,2,1,0:T(8,128)S(1)} %copy.11.pick, bf16[24,128,128]{2,1,0:T(8,128)(2,1)S(1)} %get-tuple-element.17.rest_0_, bf16[24,128,128]{2,1,0:T(8,128)(2,1)S(1)} %collective-permute-done.2.rest_1_, ...), custom_call_target="tpu_custom_call" | custom-call | flops 603979776 | bytes 12582912 | tf_op jit(solution)/shard_map/pallas_call | solution.py:331
  58.1 1.4 copy-done.2
  59.5 86.7 %shard_map.98 = (bf16[9216,128]{1,0:T(8,128)(2,1)S(1)}, bf16[9216,128]{1,0:T(8,128)(2,1)S(1)}) custom-call(bf16[9216,128]{1,0:T(8,128)(2,1)} %bitcast.7, bf16[9216,128]{1,0:T(8,128)(2,1)} %bitcast.6), custom_call_target="tpu_custom_call" | custom-call | flops 1048576 | bytes 209715200 | tf_op jit(solution)/shard_map/pallas_call | solution.py:276
  146.3 0.9 shard_map.97
  147.2 1.4 copy.16
  148.6 1.4 copy.17
  (18 shorter events, 0.1 us)
Async XLA Ops:
  0.6 14.5 %copy-start = (bf16[1,3,24,128,128]{4,3,2,1,0:T(8,128)(2,1)S(1)}, bf16[1,3,24,128,128]{4,3,2,1,0:T(8,128)(2,1)}, u32[]{:S(2)}) copy-start(bf16[1,3,24,128,128]{4,3,2,1,0:T(8,128)(2,1)} %rest_3_.5) | copy-start | bytes 7077892
  0.6 14.4 %collective-permute-start = (bf16[128,1536]{1,0:T(8,128)(2,1)}, bf16[128,1536]{1,0:T(8,128)(2,1)S(1)}, u32[]{:S(2)}, u32[]{:S(2)}) collective-permute-start(bf16[128,1536]{1,0:T(8,128)(2,1)} %rest_0_.3), channel_id=1, source_target_pairs={{0,1},{1,0},{2,3},{3,2},{4,5},{5,4},{6,7},{7,6},{8,9},{9,8},{10,11... | collective-permute-start | bytes 1179656 | tf_op jit(solution)/shard_map/ppermute | solution.py:156
  3.6 11.4 %collective-permute-start.1 = (bf16[128,1536]{1,0:T(8,128)(2,1)}, bf16[128,1536]{1,0:T(8,128)(2,1)S(1)}, u32[]{:S(2)}, u32[]{:S(2)}) collective-permute-start(bf16[128,1536]{1,0:T(8,128)(2,1)} %rest_0_.3), channel_id=1, source_target_pairs={{0,2},{1,3},{2,0},{3,1},{4,6},{5,7},{6,4},{7,5},{8,10},{9,11},{10,... | collective-permute-start | bytes 1179656 | tf_op jit(solution)/shard_map/ppermute | solution.py:156
  6.0 1.7 %copy-start.1 = (bf16[1,3,12,2,128,128]{5,4,3,2,1,0:T(8,128)(2,1)S(1)}, bf16[1,3,12,2,128,128]{5,4,3,2,1,0:T(8,128)(2,1)}, u32[]{:S(2)}) copy-start(bf16[1,3,12,2,128,128]{5,4,3,2,1,0:T(8,128)(2,1)} %weight.1) | copy-start | bytes 7077892
  7.6 1.0 copy-start.5
  8.6 6.5 %copy-start.7 = (s32[1,3,24]{2,0,1:T(1,128)S(1)}, s32[1,3,24]{2,0,1:T(1,128)}, u32[]{:S(2)}) copy-start(s32[1,3,24]{2,0,1:T(1,128)} %param.8) | copy-start | bytes 868
  8.6 6.5 %copy-start.3 = (bf16[128,1536]{1,0:T(8,128)(2,1)S(1)}, bf16[128,1536]{1,0:T(8,128)(2,1)}, u32[]{:S(2)}) copy-start(bf16[128,1536]{1,0:T(8,128)(2,1)} %rest_0_.3) | copy-start | bytes 1179652
  13.3 1.1 copy-start.4
  14.4 20.5 %collective-permute-start.4 = (bf16[24,128,128]{2,1,0:T(8,128)(2,1)S(1)}, bf16[24,128,128]{2,1,0:T(8,128)(2,1)S(1)}, u32[]{:S(2)}, u32[]{:S(2)}) collective-permute-start(bf16[24,128,128]{2,1,0:T(8,128)(2,1)S(1)} %get-tuple-element.21), channel_id=1, source_target_pairs={{0,1},{1,0},{2,3},{3,2},{4,5},{5,4},{6,7},{7,6},{8,9},{9,8},{10,11... | collective-permute-start | bytes 2359304 | tf_op jit(solution)/shard_map/ppermute | solution.py:156
  15.0 20.5 %collective-permute-start.5 = (bf16[24,128,128]{2,1,0:T(8,128)(2,1)S(1)}, bf16[24,128,128]{2,1,0:T(8,128)(2,1)S(1)}, u32[]{:S(2)}, u32[]{:S(2)}) collective-permute-start(bf16[24,128,128]{2,1,0:T(8,128)(2,1)S(1)} %get-tuple-element.22), channel_id=1, source_target_pairs={{0,2},{1,3},{2,0},{3,1},{4,6},{5,7},{6,4},{7,5},{8,10},{9,11},{10,... | collective-permute-start | bytes 2359304 | tf_op jit(solution)/shard_map/ppermute | solution.py:156
  17.8 34.0 %collective-permute-start.2 = (bf16[24,128,128]{2,1,0:T(8,128)(2,1)S(1)}, bf16[24,128,128]{2,1,0:T(8,128)(2,1)S(1)}, u32[]{:S(2)}, u32[]{:S(2)}) collective-permute-start(bf16[24,128,128]{2,1,0:T(8,128)(2,1)S(1)} %get-tuple-element.17.rest_0_), channel_id=1, source_target_pairs={{0,1},{1,0},{2,3},{3,2},{4,5},{5,4},{6,7},{7,6},{8,9},{9,8},{10,11... | collective-permute-start | bytes 2359304 | tf_op jit(solution)/shard_map/ppermute | solution.py:156
  19.8 32.6 %collective-permute-start.3 = (bf16[24,128,128]{2,1,0:T(8,128)(2,1)S(1)}, bf16[24,128,128]{2,1,0:T(8,128)(2,1)S(1)}, u32[]{:S(2)}, u32[]{:S(2)}) collective-permute-start(bf16[24,128,128]{2,1,0:T(8,128)(2,1)S(1)} %get-tuple-element.17.rest_0_), channel_id=1, source_target_pairs={{0,2},{1,3},{2,0},{3,1},{4,6},{5,7},{6,4},{7,5},{8,10},{9,11},{10,... | collective-permute-start | bytes 2359304 | tf_op jit(solution)/shard_map/ppermute | solution.py:156
  35.5 16.9 %copy-start.6 = (bf16[128,1536]{1,0:T(8,128)(2,1)S(1)}, bf16[128,1536]{1,0:T(8,128)(2,1)}, u32[]{:S(2)}) copy-start(bf16[128,1536]{1,0:T(8,128)(2,1)} %dy.1) | copy-start | bytes 1179652
  44.9 101.3 %collective-permute-start.6 = (bf16[12,128,128]{2,1,0:T(8,128)(2,1)S(1)}, bf16[12,128,128]{2,1,0:T(8,128)(2,1)S(1)}, u32[]{:S(2)}, u32[]{:S(2)}) collective-permute-start(bf16[12,128,128]{2,1,0:T(8,128)(2,1)S(1)} %get-tuple-element.24), channel_id=1, source_target_pairs={{0,1},{1,0},{2,3},{3,2},{4,5},{5,4},{6,7},{7,6},{8,9},{9,8},{10,11... | collective-permute-start | bytes 1179656 | tf_op jit(solution)/shard_map/ppermute | solution.py:156
  46.4 99.9 %collective-permute-start.7 = (bf16[12,128,128]{2,1,0:T(8,128)(2,1)S(1)}, bf16[12,128,128]{2,1,0:T(8,128)(2,1)S(1)}, u32[]{:S(2)}, u32[]{:S(2)}) collective-permute-start(bf16[12,128,128]{2,1,0:T(8,128)(2,1)S(1)} %get-tuple-element.25), channel_id=1, source_target_pairs={{0,2},{1,3},{2,0},{3,1},{4,6},{5,7},{6,4},{7,5},{8,10},{9,11},{10,... | collective-permute-start | bytes 1179656 | tf_op jit(solution)/shard_map/ppermute | solution.py:156
  58.1 1.4 copy-start.2

commit v6 on v5

--- a/solution.py
+++ b/solution.py
@@ -177,7 +177,7 @@
 
 
 def stream_count(rows, devices):
-    return next((n for n in (6, 4, 3, 2, 1) if rows % (16 * devices * n) == 0), 0)
+    return next((n for n in (8, 6, 4, 3, 2, 1) if rows % (16 * devices * n) == 0), 0)
 
 
 def sum_streams_body(count, streams, bits, scale, *refs):

time: 150 us -> 152 us (1.013)
  Pallas kernels: 110 us -> 112 us
where the time goes in v6:
time: 152 us; the launch traced here: 151 us
  Pallas kernels  112 us (74%)
  waiting for transfers between devices  19.6 us (13%)
  starting transfers between devices  10.6 us (7%)
  local copies, waits for them, and re-layouts  8.81 us (6%)
    pallas_call x1, Pallas kernels, token_sums(): pl.pallas_call(functools.partial(sum_streams_body, count, streams, bits,...  88 us
    ppermute x8, waiting for transfers between devices, swap(): return lax.ppermute(block, axis, [(i, i ^ 1 << bit) for i in range(count)])  19.6 us
    ppermute x8, starting transfers between devices, swap(): return lax.ppermute(block, axis, [(i, i ^ 1 << bit) for i in range(count)])  10.6 us
    pallas_call x1, Pallas kernels, local(): call(functools.partial(mid_body, levels), [((levels, hid_blocks, size, si...  9.48 us
    unnamed x20, local copies, waits for them, and re-layouts  8.81 us
    pallas_call x1, Pallas kernels, local(): call(functools.partial(down_body, levels), [((tokens, width), BF16), ((le...  5.8 us
    pallas_call x1, Pallas kernels, local(): call(functools.partial(back_body, levels), [(hid, F32)] + [(hid, BF16)] *...  4.68 us
  transfers between devices with their start and end apart: 8, of which 4 were waited for; matrix products, arithmetic and copies ran while one was open for 1% of the time, Pallas kernels for 73%

profile of v6, /device:TPU:0, one launch (start us, length us, event | category | flops | bytes accessed | tf_op | source)
XLA Modules:
  0.0 151.3 jit_solution(6612365495650746499)
XLA Ops:
  0.6 3.0 %collective-permute-start = (bf16[128,1536]{1,0:T(8,128)(2,1)}, bf16[128,1536]{1,0:T(8,128)(2,1)S(1)}, u32[]{:S(2)}, u32[]{:S(2)}) collective-permute-start(bf16[128,1536]{1,0:T(8,128)(2,1)} %rest_0_.3), channel_id=1, source_target_pairs={{0,1},{1,0},{2,3},{3,2},{4,5},{5,4},{6,7},{7,6},{8,9},{9,8},{10,11... | collective-permute-start | bytes 1179656 | tf_op jit(solution)/shard_map/ppermute | solution.py:156
  3.6 1.5 %collective-permute-start.1 = (bf16[128,1536]{1,0:T(8,128)(2,1)}, bf16[128,1536]{1,0:T(8,128)(2,1)S(1)}, u32[]{:S(2)}, u32[]{:S(2)}) collective-permute-start(bf16[128,1536]{1,0:T(8,128)(2,1)} %rest_0_.3), channel_id=1, source_target_pairs={{0,2},{1,3},{2,0},{3,1},{4,6},{5,7},{6,4},{7,5},{8,10},{9,11},{10,... | collective-permute-start | bytes 1179656 | tf_op jit(solution)/shard_map/ppermute | solution.py:156
  5.2 0.8 copy.11.pick
  6.0 1.7 %copy-done.1 = bf16[1,3,12,2,128,128]{5,4,3,2,1,0:T(8,128)(2,1)S(1)} copy-done((bf16[1,3,12,2,128,128]{5,4,3,2,1,0:T(8,128)(2,1)S(1)}, bf16[1,3,12,2,128,128]{5,4,3,2,1,0:T(8,128)(2,1)}, u32[]{:S(2)}) %copy-start.1) | copy-done | bytes 2359320
  7.6 1.0 copy-done.5
  8.6 4.7 %shard_map.95 = (f32[24,128,128]{2,1,0:T(8,128)S(1)}, bf16[24,128,128]{2,1,0:T(8,128)(2,1)S(1)}, bf16[24,128,128]{2,1,0:T(8,128)(2,1)S(1)}) custom-call(s32[1,3,12,2]{3,2,1,0:T(8,128)S(1)} %copy.11.pick, bf16[128,1536]{1,0:T(8,128)(2,1)S(1)} %copy-done.5, bf16[1,3,12,2,128,128]{5,4,3,2,1,0:T(8,128)(2,1)S(1)} %copy-done.1), custom_call_target="tpu_custom_call" | custom-call | flops 301989888 | bytes 8388608 | tf_op jit(solution)/shard_map/pallas_call | solution.py:308
  13.3 1.1 copy-done.4
  14.4 0.5 collective-permute-start.4
  15.1 2.7 %shard_map.93 = (f32[24,128,128]{2,1,0:T(8,128)S(1)}, bf16[24,128,128]{2,1,0:T(8,128)(2,1)S(1)}) custom-call(s32[1,3,24]{2,1,0:T(4,128)S(1)} %copy.10.pick, bf16[128,1536]{1,0:T(8,128)(2,1)S(1)} %copy-done.3, bf16[128,1536]{1,0:T(8,128)(2,1)S(1)} %collective-permute-done.rest_1_, bf16[128,1536]{1,0:T(8,128)(2,1)S(1)} %collective-permute-done.1.rest_2_, ...), custom_call_target="tpu_custom_call" | custom-call | flops 301989888 | bytes 8388608 | tf_op jit(solution)/shard_map/pallas_call | solution.py:315
  17.8 2.0 %collective-permute-start.2 = (bf16[24,128,128]{2,1,0:T(8,128)(2,1)S(1)}, bf16[24,128,128]{2,1,0:T(8,128)(2,1)S(1)}, u32[]{:S(2)}, u32[]{:S(2)}) collective-permute-start(bf16[24,128,128]{2,1,0:T(8,128)(2,1)S(1)} %get-tuple-element.17.rest_0_), channel_id=1, source_target_pairs={{0,1},{1,0},{2,3},{3,2},{4,5},{5,4},{6,7},{7,6},{8,9},{9,8},{10,11... | collective-permute-start | bytes 2359304 | tf_op jit(solution)/shard_map/ppermute | solution.py:156
  19.8 1.5 collective-permute-start.3
  21.3 13.7 %collective-permute-done.4.rest_6_ = bf16[24,128,128]{2,1,0:T(8,128)(2,1)S(1)} collective-permute-done((bf16[24,128,128]{2,1,0:T(8,128)(2,1)S(1)}, bf16[24,128,128]{2,1,0:T(8,128)(2,1)S(1)}, u32[]{:S(2)}, u32[]{:S(2)}) %collective-permute-start.4) | collective-permute-done | bytes 786464 | tf_op jit(solution)/shard_map/ppermute | solution.py:156
  34.9 0.5 collective-permute-done.5.rest_7_
  35.5 9.5 %shard_map.96 = (bf16[3,24,128,128]{3,2,1,0:T(8,128)(2,1)}, f32[12,128,128]{2,1,0:T(8,128)S(1)}, bf16[12,128,128]{2,1,0:T(8,128)(2,1)S(1)}, bf16[12,128,128]{2,1,0:T(8,128)(2,1)S(1)}) custom-call(s32[1,3,24]{2,1,0:T(4,128)S(1)} %copy.10.pick, bf16[128,1536]{1,0:T(8,128)(2,1)S(1)} %copy-done.3, bf16[128,1536]{1,0:T(8,128)(2,1)S(1)} %collective-permute-done.rest_1_, ...), custom_call_target="tpu_custom_call" | custom-call | flops 603979776 | bytes 16777216 | tf_op jit(solution)/shard_map/pallas_call | solution.py:321
  44.9 1.4 collective-permute-start.6
  46.4 0.5 collective-permute-start.7
  46.9 4.9 %collective-permute-done.2.rest_1_ = bf16[24,128,128]{2,1,0:T(8,128)(2,1)S(1)} collective-permute-done((bf16[24,128,128]{2,1,0:T(8,128)(2,1)S(1)}, bf16[24,128,128]{2,1,0:T(8,128)(2,1)S(1)}, u32[]{:S(2)}, u32[]{:S(2)}) %collective-permute-start.2) | collective-permute-done | bytes 786464 | tf_op jit(solution)/shard_map/ppermute | solution.py:156
  51.8 0.5 collective-permute-done.3.rest_2_
  52.3 5.8 %shard_map.94 = (bf16[128,1536]{1,0:T(8,128)(2,1)}, bf16[3,12,2,128,128]{4,3,2,1,0:T(8,128)(2,1)S(1)}) custom-call(s32[1,3,12,2]{3,2,1,0:T(8,128)S(1)} %copy.11.pick, bf16[24,128,128]{2,1,0:T(8,128)(2,1)S(1)} %get-tuple-element.17.rest_0_, bf16[24,128,128]{2,1,0:T(8,128)(2,1)S(1)} %collective-permute-done.2.rest_1_, ...), custom_call_target="tpu_custom_call" | custom-call | flops 603979776 | bytes 12582912 | tf_op jit(solution)/shard_map/pallas_call | solution.py:331
  58.1 1.4 copy-done.2
  59.5 88.0 %shard_map.98 = (bf16[9216,128]{1,0:T(8,128)(2,1)S(1)}, bf16[9216,128]{1,0:T(8,128)(2,1)S(1)}) custom-call(bf16[9216,128]{1,0:T(8,128)(2,1)} %bitcast.7, bf16[9216,128]{1,0:T(8,128)(2,1)} %bitcast.6), custom_call_target="tpu_custom_call" | custom-call | flops 1048576 | bytes 209715200 | tf_op jit(solution)/shard_map/pallas_call | solution.py:276
  147.6 0.9 shard_map.97
  148.5 1.4 copy.16
  149.9 1.4 copy.17
  (18 shorter events, 0.1 us)
Async XLA Ops:
  0.6 14.5 %copy-start = (bf16[1,3,24,128,128]{4,3,2,1,0:T(8,128)(2,1)S(1)}, bf16[1,3,24,128,128]{4,3,2,1,0:T(8,128)(2,1)}, u32[]{:S(2)}) copy-start(bf16[1,3,24,128,128]{4,3,2,1,0:T(8,128)(2,1)} %rest_3_.5) | copy-start | bytes 7077892
  0.6 14.4 %collective-permute-start = (bf16[128,1536]{1,0:T(8,128)(2,1)}, bf16[128,1536]{1,0:T(8,128)(2,1)S(1)}, u32[]{:S(2)}, u32[]{:S(2)}) collective-permute-start(bf16[128,1536]{1,0:T(8,128)(2,1)} %rest_0_.3), channel_id=1, source_target_pairs={{0,1},{1,0},{2,3},{3,2},{4,5},{5,4},{6,7},{7,6},{8,9},{9,8},{10,11... | collective-permute-start | bytes 1179656 | tf_op jit(solution)/shard_map/ppermute | solution.py:156
  3.6 11.4 %collective-permute-start.1 = (bf16[128,1536]{1,0:T(8,128)(2,1)}, bf16[128,1536]{1,0:T(8,128)(2,1)S(1)}, u32[]{:S(2)}, u32[]{:S(2)}) collective-permute-start(bf16[128,1536]{1,0:T(8,128)(2,1)} %rest_0_.3), channel_id=1, source_target_pairs={{0,2},{1,3},{2,0},{3,1},{4,6},{5,7},{6,4},{7,5},{8,10},{9,11},{10,... | collective-permute-start | bytes 1179656 | tf_op jit(solution)/shard_map/ppermute | solution.py:156
  6.0 1.7 %copy-start.1 = (bf16[1,3,12,2,128,128]{5,4,3,2,1,0:T(8,128)(2,1)S(1)}, bf16[1,3,12,2,128,128]{5,4,3,2,1,0:T(8,128)(2,1)}, u32[]{:S(2)}) copy-start(bf16[1,3,12,2,128,128]{5,4,3,2,1,0:T(8,128)(2,1)} %weight.1) | copy-start | bytes 7077892
  7.6 1.0 copy-start.5
  8.6 6.5 %copy-start.7 = (s32[1,3,24]{2,0,1:T(1,128)S(1)}, s32[1,3,24]{2,0,1:T(1,128)}, u32[]{:S(2)}) copy-start(s32[1,3,24]{2,0,1:T(1,128)} %param.8) | copy-start | bytes 868
  8.6 6.5 %copy-start.3 = (bf16[128,1536]{1,0:T(8,128)(2,1)S(1)}, bf16[128,1536]{1,0:T(8,128)(2,1)}, u32[]{:S(2)}) copy-start(bf16[128,1536]{1,0:T(8,128)(2,1)} %rest_0_.3) | copy-start | bytes 1179652
  13.3 1.1 copy-start.4
  14.4 20.5 %collective-permute-start.4 = (bf16[24,128,128]{2,1,0:T(8,128)(2,1)S(1)}, bf16[24,128,128]{2,1,0:T(8,128)(2,1)S(1)}, u32[]{:S(2)}, u32[]{:S(2)}) collective-permute-start(bf16[24,128,128]{2,1,0:T(8,128)(2,1)S(1)} %get-tuple-element.21), channel_id=1, source_target_pairs={{0,1},{1,0},{2,3},{3,2},{4,5},{5,4},{6,7},{7,6},{8,9},{9,8},{10,11... | collective-permute-start | bytes 2359304 | tf_op jit(solution)/shard_map/ppermute | solution.py:156
  15.0 20.5 %collective-permute-start.5 = (bf16[24,128,128]{2,1,0:T(8,128)(2,1)S(1)}, bf16[24,128,128]{2,1,0:T(8,128)(2,1)S(1)}, u32[]{:S(2)}, u32[]{:S(2)}) collective-permute-start(bf16[24,128,128]{2,1,0:T(8,128)(2,1)S(1)} %get-tuple-element.22), channel_id=1, source_target_pairs={{0,2},{1,3},{2,0},{3,1},{4,6},{5,7},{6,4},{7,5},{8,10},{9,11},{10,... | collective-permute-start | bytes 2359304 | tf_op jit(solution)/shard_map/ppermute | solution.py:156
  17.8 34.0 %collective-permute-start.2 = (bf16[24,128,128]{2,1,0:T(8,128)(2,1)S(1)}, bf16[24,128,128]{2,1,0:T(8,128)(2,1)S(1)}, u32[]{:S(2)}, u32[]{:S(2)}) collective-permute-start(bf16[24,128,128]{2,1,0:T(8,128)(2,1)S(1)} %get-tuple-element.17.rest_0_), channel_id=1, source_target_pairs={{0,1},{1,0},{2,3},{3,2},{4,5},{5,4},{6,7},{7,6},{8,9},{9,8},{10,11... | collective-permute-start | bytes 2359304 | tf_op jit(solution)/shard_map/ppermute | solution.py:156
  19.8 32.6 %collective-permute-start.3 = (bf16[24,128,128]{2,1,0:T(8,128)(2,1)S(1)}, bf16[24,128,128]{2,1,0:T(8,128)(2,1)S(1)}, u32[]{:S(2)}, u32[]{:S(2)}) collective-permute-start(bf16[24,128,128]{2,1,0:T(8,128)(2,1)S(1)} %get-tuple-element.17.rest_0_), channel_id=1, source_target_pairs={{0,2},{1,3},{2,0},{3,1},{4,6},{5,7},{6,4},{7,5},{8,10},{9,11},{10,... | collective-permute-start | bytes 2359304 | tf_op jit(solution)/shard_map/ppermute | solution.py:156
  35.5 16.9 %copy-start.6 = (bf16[128,1536]{1,0:T(8,128)(2,1)S(1)}, bf16[128,1536]{1,0:T(8,128)(2,1)}, u32[]{:S(2)}) copy-start(bf16[128,1536]{1,0:T(8,128)(2,1)} %dy.1) | copy-start | bytes 1179652
  44.9 102.6 %collective-permute-start.6 = (bf16[12,128,128]{2,1,0:T(8,128)(2,1)S(1)}, bf16[12,128,128]{2,1,0:T(8,128)(2,1)S(1)}, u32[]{:S(2)}, u32[]{:S(2)}) collective-permute-start(bf16[12,128,128]{2,1,0:T(8,128)(2,1)S(1)} %get-tuple-element.24), channel_id=1, source_target_pairs={{0,1},{1,0},{2,3},{3,2},{4,5},{5,4},{6,7},{7,6},{8,9},{9,8},{10,11... | collective-permute-start | bytes 1179656 | tf_op jit(solution)/shard_map/ppermute | solution.py:156
  46.4 101.2 %collective-permute-start.7 = (bf16[12,128,128]{2,1,0:T(8,128)(2,1)S(1)}, bf16[12,128,128]{2,1,0:T(8,128)(2,1)S(1)}, u32[]{:S(2)}, u32[]{:S(2)}) collective-permute-start(bf16[12,128,128]{2,1,0:T(8,128)(2,1)S(1)} %get-tuple-element.25), channel_id=1, source_target_pairs={{0,2},{1,3},{2,0},{3,1},{4,6},{5,7},{6,4},{7,5},{8,10},{9,11},{10,... | collective-permute-start | bytes 1179656 | tf_op jit(solution)/shard_map/ppermute | solution.py:156
  58.1 1.4 copy-start.2
